TPU v7x, 32 devices: a whole 2x2x4 slice. The times are simulated.
32 devices in a mesh: seg: 2 (over y), row: 4 (over x, core), col: 4 (over z).
Axes of the slice: x: 2, y: 2, z: 4, core: 2. Of those that a mesh axis runs over, the one named last changes fastest.
Arguments:
- raw_traces: bfloat16 [8192, 16, 256], P(('seg', 'row', 'col')), parts along dimension 0, may hold values from -6 to 6
- channel_pick: int32 [4096], P(('seg', 'row', 'col')), parts along dimension 0, may hold values from 0 to 4095, as said below
- clip_mask: int32 [4096, 16], P(('seg', 'row', 'col')), parts along dimension 0, may hold values 0 or 1
Outputs:
- correlations: bfloat16 [4096, 2048, 128], P(('seg', 'row'), 'col'), parts along dimension 0
There are 2 independent parts, one for each index of `seg`. A program takes and returns all parts, laid end to end along the dimension named above; each array names one. Nothing has to cross between parts.
Inputs may be any that keep to these rules, and one draw needn't show every extreme that they name: `channel_pick`: entry j is 2j or 2j+1; entry 0 is even and entry 2047 is odd.
All inputs are finite; a program needn't handle non-finite values. No bound on the sum of `clip_mask` on one device may be relied on, other than what follows from the above.
Results may differ from a plain program's by a relative error of at most 0.0057.
Values may be sent and summed in bfloat16 or wider, within the bound.
No kernel may reach another device: no remote copies, remote signals or barrier semaphores. Data moves between devices by JAX's collectives and lax.ppermute only.
A program may use at most 576 MiB of HBM per device.

v0:
```python
import math

import jax
import jax.numpy as jnp
from jax import lax
from jax.sharding import PartitionSpec as P

L = 128


def broadcast(value, axis, source):
    kept = jnp.where(lax.axis_index(axis) == source, value, 0).astype(value.dtype)
    return lax.psum(kept, axis)


def whiten_block(picked, keep):
    samples = picked.shape[2]
    half = samples // 2
    pos = jnp.arange(samples, dtype=jnp.int32)
    freq = jnp.arange(1, half + 1, dtype=jnp.int32)
    phase = pos[:, None] * freq[None, :] % samples
    angle = phase.astype(jnp.float32) * (2.0 * math.pi / samples)
    table = jnp.concatenate([jnp.cos(angle), -jnp.sin(angle)], axis=1)
    flat = picked.astype(jnp.float32).reshape(-1, samples)
    spec = jnp.dot(flat, table, precision=lax.Precision.HIGHEST, preferred_element_type=jnp.float32)
    real_part = spec[:, :half]
    imag_part = spec[:, half:]
    power = real_part * real_part + imag_part * imag_part
    gap = jnp.abs(freq[:, None] - freq[None, :])
    band = jnp.where(gap <= 2, 0.2, 0.0).astype(jnp.float32)
    smooth = jnp.dot(
        power, band, precision=lax.Precision.HIGHEST, preferred_element_type=jnp.float32
    )
    denom = jnp.sqrt(smooth + 0.1 * jnp.mean(power, axis=1, keepdims=True) + 1e-06)
    weight = keep.reshape(-1, 1).astype(jnp.float32) / denom
    whitened = jnp.concatenate([real_part * weight, imag_part * weight], axis=1)
    return whitened.astype(jnp.bfloat16).reshape(picked.shape[0], picked.shape[1], samples)


def lag_tables(half, samples, lags, windows):
    freq = jnp.arange(1, half + 1, dtype=jnp.int32)
    shift = jnp.arange(lags, dtype=jnp.int32) - lags // 2
    phase = freq[:, None] * shift[None, :] % samples
    angle = phase.astype(jnp.float32) * (2.0 * math.pi / samples)
    scale = 1.0 / math.sqrt(windows * half)
    return (jnp.cos(angle) * scale, jnp.sin(angle) * scale)


def local(raw_traces, channel_pick, clip_mask):
    owned = channel_pick.shape[0]
    windows = raw_traces.shape[1]
    samples = raw_traces.shape[2]
    half = samples // 2
    paired = raw_traces.reshape(owned, 2, windows, samples)
    parity = (channel_pick % 2)[:, None, None]
    picked = jnp.where(parity == 1, paired[:, 1], paired[:, 0])
    diagonal = lax.axis_index("col")
    outgoing = whiten_block(picked, clip_mask)
    row_first, row_keep = (
        lax.all_gather(outgoing, "col", axis=0, tiled=True),
        lax.all_gather(clip_mask, "col", axis=0, tiled=True),
    )
    col_first, col_keep = (
        broadcast(row_first, "row", diagonal),
        broadcast(row_keep, "row", diagonal),
    )
    tile = row_first.shape[0]
    lags = L
    rotated = jnp.concatenate([-col_first[:, :, half:], col_first[:, :, :half]], axis=2)
    row_four = row_first.reshape(tile, windows, 2, half)
    col_four = col_first.reshape(tile, windows, 2, half)
    rot_four = rotated.reshape(tile, windows, 2, half)
    cross_re = jnp.einsum("iwpk,jwpk->ijk", row_four, col_four, preferred_element_type=jnp.float32)
    cross_im = jnp.einsum("iwpk,jwpk->ijk", row_four, rot_four, preferred_element_type=jnp.float32)
    cos_table, sin_table = lag_tables(half, samples, lags, windows)
    lagged = jnp.dot(
        cross_re.reshape(-1, half),
        cos_table,
        precision=lax.Precision.HIGHEST,
        preferred_element_type=jnp.float32,
    )
    lagged = lagged - jnp.dot(
        cross_im.reshape(-1, half),
        sin_table,
        precision=lax.Precision.HIGHEST,
        preferred_element_type=jnp.float32,
    )
    lagged = lagged.reshape(tile, tile, lags)
    row_ids = lax.axis_index("row") * tile + jnp.arange(tile, dtype=jnp.int32)
    col_ids = diagonal * tile + jnp.arange(tile, dtype=jnp.int32)
    same = row_ids[:, None] == col_ids[None, :]
    return jnp.where(same[:, :, None], 0.0, lagged).astype(jnp.bfloat16)


def solution(mesh):
    return jax.shard_map(
        local,
        mesh=mesh,
        in_specs=(
            P(("seg", "row", "col"), None, None),
            P(("seg", "row", "col")),
            P(("seg", "row", "col"), None),
        ),
        out_specs=P(("seg", "row"), "col", None),
        check_vma=False,
    )
```

profile of v0, /device:TPU:0, one launch (start us, length us, event | category | flops | bytes accessed | tf_op | source)
XLA Modules:
  0.0 1067.3 jit_solution(9108566769542848185)
XLA Ops:
  6.5 0.0 copy-start.5
  6.5 0.0 all-gather.2.cloned.1.call-start
  6.5 0.6 iota_add_fusion.2
  7.1 0.0 copy-start.2
  7.1 0.5 fusion.27
  7.7 1.7 fusion.53
  9.4 0.0 copy-done.5
  9.4 0.1 broadcast_in_dim.49
  9.5 0.1 broadcast_in_dim.50
  9.6 0.0 copy-start.1
  9.6 0.6 bitcast_select_fusion
  10.2 1.0 fusion.7
  11.2 0.3 fusion.11
  11.6 0.0 copy-done.1
  11.6 0.1 copy.4
  11.7 0.1 convert_element_type.31
  11.8 0.0 copy-done.2
  11.8 1.5 multiply_convert_fusion.1
  13.3 0.5 copy.5
  13.8 0.5 copy.6
  14.3 1.0 pad_maximum_fusion.1
  15.3 0.0 all-gather.2.cloned.1.call-update
  15.3 0.2 all-reduce.2.cloned.1.call-start
  15.6 83.2 %all-gather.2.cloned.1.call-done = bf16[512,16,256]{0,2,1:T(8,128)(2,1)} async-done(((bf16[128,16,256]{0,2,1:T(8,128)(2,1)}), bf16[512,16,256]{0,2,1:T(8,128)(2,1)}) %all-gather.2.cloned.1.call-update) | async-done | bytes 4194320 | tf_op jit(solution)/shard_map/all_gather | solution.py:60
  98.8 4.5 broadcast_select_fusion
  103.2 0.0 all-reduce.2.cloned.1.call-update
  103.3 0.9 broadcast_compare_fusion
  104.2 82.9 %all-reduce.2.cloned.1.call-done = bf16[512,16,256]{0,2,1:T(8,128)(2,1)} async-done(((bf16[512,16,256]{0,2,1:T(8,128)(2,1)}), bf16[512,16,256]{0,2,1:T(8,128)(2,1)}) %all-reduce.2.cloned.1.call-update) | async-done | bytes 4194320 | tf_op jit(solution)/shard_map/psum | solution.py:13
  187.1 48.9 %convolution_bitcast_fusion.1 = f32[512,512,128]{0,1,2:T(8,128)} fusion(bf16[512,16,2,128]{0,3,2,1:T(8,128)(2,1)} %bitcast.30, bf16[512,16,2,128]{0,3,2,1:T(8,128)(2,1)} %bitcast.28), kind=kOutput, calls=%fused_computation.3 | convolution fusion | flops 2147483648 | bytes 142606336 | tf_op jit(solution)/shard_map/iwpk,jwpk->ijk/dot_general | solution.py:73
  236.0 134.1 %copy.9 = f32[512,512,128]{2,1,0:T(8,128)} copy(f32[512,512,128]{0,1,2:T(8,128)} %convolution_bitcast_fusion.1) | data formatting | bytes 268435456 | tf_op jit(solution)/shard_map/iwpk,jwpk->ijk/transpose | solution.py:73
  370.0 2.5 slice_negate_fusion
  372.5 2.4 pad_maximum_fusion
  374.9 48.9 %convolution_bitcast_fusion = f32[512,512,128]{0,1,2:T(8,128)} fusion(bf16[512,16,2,128]{0,3,2,1:T(8,128)(2,1)} %bitcast.31, bf16[512,16,2,128]{0,3,2,1:T(8,128)(2,1)} %bitcast.29), kind=kOutput, calls=%fused_computation.2 | convolution fusion | flops 2147483648 | bytes 142606336 | tf_op jit(solution)/shard_map/iwpk,jwpk->ijk/dot_general | solution.py:74
  423.8 0.0 copy-start.3
  423.8 0.0 copy-start.4
  423.8 134.1 %copy.12 = f32[512,512,128]{2,1,0:T(8,128)} copy(f32[512,512,128]{0,1,2:T(8,128)} %convolution_bitcast_fusion) | data formatting | bytes 268435456 | tf_op jit(solution)/shard_map/iwpk,jwpk->ijk/transpose | solution.py:74
  557.9 0.0 copy-done.3
  557.9 0.0 copy-done.4
  557.9 224.6 %fusion.23 = f32[262144,128]{1,0:T(8,128)} fusion(f32[262144,128]{1,0:T(8,128)} %bitcast.10, s32[128]{0:T(128)S(1)} %copy-done.4, s32[128]{0:T(128)S(1)} %copy-done.3), kind=kOutput, calls=%fused_computation.46 | convolution fusion | flops 51539853312 | bytes 268436480 | tf_op jit(solution)/shard_map/dot_general | solution.py:76
  782.5 0.0 copy-start
  782.5 228.1 %convolution_subtract_fusion = bf16[262144,128]{1,0:T(8,128)(2,1)} fusion(f32[262144,128]{1,0:T(8,128)} %fusion.23, f32[262144,128]{1,0:T(8,128)} %bitcast.15, s32[128]{0:T(128)S(1)} %copy-done.4, s32[128]{0:T(128)S(1)} %copy-done.3), kind=kOutput, calls=%fused_computation | convolution fusion | flops 51606962176 | bytes 335545344 | tf_op jit(solution)/shard_map/dot_general | solution.py:82
  1010.6 0.0 copy-done
  1010.6 49.9 %select_convert_fusion = bf16[512,512,128]{2,1,0:T(8,128)(2,1)} fusion(bf16[512,512,128]{2,1,0:T(8,128)(2,1)} %bitcast.16, pred[512,512]{1,0:T(8,128)(4,1)S(1)} %copy-done), kind=kLoop, calls=%fused_computation.1 | loop fusion | flops 33554432 | bytes 134479872 | tf_op jit(solution)/shard_map/convert_element_type | solution.py:92
  (4 shorter events, 0.0 us)
Async XLA Ops:
  6.5 2.8 copy-start.5
  6.5 92.2 %all-gather.2.cloned.1.call-start = ((), (), s32[]{:S(2)}) async-start(), calls=%async_computation | async-start | bytes 5242880 | tf_op jit(solution)/shard_map/all_gather | solution.py:60
  7.1 4.7 copy-start.2
  9.6 2.0 copy-start.1
  15.3 171.8 %all-reduce.2.cloned.1.call-start = ((), (), s32[]{:S(2)}) async-start(), calls=%async_computation.1 | async-start | bytes 8388608 | tf_op jit(solution)/shard_map/psum | solution.py:13
  423.8 134.1 %copy-start.3 = (s32[128]{0:T(128)S(1)}, s32[128]{0:T(128)}, u32[]{:S(2)}) copy-start(s32[128]{0:T(128)} %copy-done.2) | copy-start | bytes 1540
  423.8 134.1 %copy-start.4 = (s32[128]{0:T(128)S(1)}, s32[128]{0:T(128)}, u32[]{:S(2)}) copy-start(s32[128]{0:T(128)} %get-tuple-element.13) | copy-start | bytes 1540
  782.5 228.1 %copy-start = (pred[512,512]{1,0:T(8,128)(4,1)S(1)}, pred[512,512]{1,0:T(8,128)(4,1)}, u32[]{:S(2)}) copy-start(pred[512,512]{1,0:T(8,128)(4,1)} %broadcast_compare_fusion) | copy-start | bytes 786436
Sparse Core Ops, SparseCore 0:
  15.4 83.2 all-gather.1
  103.4 83.6 all-reduce.1
where the time goes:
time: 1070 us
  matrix products  553 us (52%)
  local copies, waits for them, and re-layouts  271 us (25%)
  waiting for transfers between devices  166 us (16%)
  other arithmetic  63.3 us (6%)
  between operations  13.5 us (1%)
    dot_general x1, matrix products, local(): jnp.dot(cross_im.reshape(-1, half), sin_table, precision=lax.Precision.HI...  228 us
    dot_general x1, matrix products, local(): jnp.dot(cross_re.reshape(-1, half), cos_table, precision=lax.Precision.HI...  225 us
    transpose x1, local copies, waits for them, and re-layouts, local(): jnp.einsum('iwpk,jwpk->ijk', row_four, rot_four, preferred_element_type=j...  134 us
    transpose x1, local copies, waits for them, and re-layouts, local(): jnp.einsum('iwpk,jwpk->ijk', row_four, col_four, preferred_element_type=j...  134 us
    all_gather x1, waiting for transfers between devices, local(): lax.all_gather(outgoing, 'col', axis=0, tiled=True)  83.2 us
    psum x1, waiting for transfers between devices, broadcast(): return lax.psum(kept, axis)  82.9 us
    convert_element_type x1, other arithmetic, local(): return jnp.where(same[:, :, None], 0.0, lagged).astype(jnp.bfloat16)  49.9 us
    dot_general x1, matrix products, local(): jnp.einsum('iwpk,jwpk->ijk', row_four, rot_four, preferred_element_type=j...  48.9 us
  transfers between devices with their start and end apart: 2, of which 2 were waited for; matrix products, arithmetic and copies ran while one was open for 0% of the time, Pallas kernels for 0%

commit v1 on v0

v1 whole, which is shorter than its diff:
```python
import functools
import math

import jax
import jax.numpy as jnp
import ml_dtypes
import numpy as np
from jax import lax
from jax.experimental import pallas as pl
from jax.experimental.pallas import tpu as pltpu
from jax.sharding import PartitionSpec as P

L = 128
LANES = 128
PAD = 8


def spectrum_tables(samples):
    half = samples // 2
    freq = np.arange(1, half + 1)
    pos = np.arange(samples)
    angle = (freq[:, None] * pos[None, :] % samples) * (2.0 * np.pi / samples)
    table = np.concatenate([np.cos(angle), -np.sin(angle)], axis=0).astype(np.float32)
    high = table.astype(ml_dtypes.bfloat16)
    low = (table - high.astype(np.float32)).astype(ml_dtypes.bfloat16)
    return high, low


def lag_table(samples, lags, windows):
    half = samples // 2
    freq = np.arange(1, half + 1)
    shift = np.arange(lags) - lags // 2
    angle = (freq[:, None] * shift[None, :] % samples) * (2.0 * np.pi / samples)
    scale = 1.0 / math.sqrt(windows * half)
    table = np.concatenate([np.cos(angle), -np.sin(angle)], axis=0) * scale
    return table.astype(ml_dtypes.bfloat16)


def whiten_kernel(raw_ref, keep_ref, high_ref, low_ref, z_ref, rows_ref):
    windows = raw_ref.shape[0]
    half = high_ref.shape[0] // 2
    parts = 2 * windows
    pitch = parts + PAD
    contract = (((1,), (1,)), ((), ()))

    def window(w, carry):
        raw = raw_ref[w]
        spec = lax.dot_general(high_ref[...], raw, contract, preferred_element_type=jnp.float32)
        spec += lax.dot_general(low_ref[...], raw, contract, preferred_element_type=jnp.float32)
        real, imag = spec[:half], spec[half:]
        power = real * real + imag * imag
        total = power
        for gap in (1, 2):
            edge = jnp.zeros((gap, power.shape[1]), jnp.float32)
            total += jnp.concatenate([power[gap:], edge], axis=0)
            total += jnp.concatenate([edge, power[:-gap]], axis=0)
        mean = jnp.sum(power, axis=0, keepdims=True) * (1.0 / half)
        denom = jnp.sqrt(total * 0.2 + 0.1 * mean + 1e-06)
        weight = keep_ref[pl.ds(w, 1), :] / denom
        rows_ref[pl.ds(w, half, stride=pitch), :] = real * weight
        rows_ref[pl.ds(windows + w, half, stride=pitch), :] = imag * weight
        return carry

    lax.fori_loop(0, windows, window, 0, unroll=4)

    def narrow(k, carry):
        start = pl.multiple_of(k * pitch, 8)
        z_ref[k] = rows_ref[pl.ds(start, parts), :].astype(jnp.bfloat16)
        return carry

    lax.fori_loop(0, half, narrow, 0, unroll=8)


def whiten(picked, keep):
    windows, channels, samples = picked.shape
    half = samples // 2
    high, low = spectrum_tables(samples)
    return pl.pallas_call(
        whiten_kernel,
        grid=(channels // LANES,),
        in_specs=[
            pl.BlockSpec((windows, LANES, samples), lambda c: (0, c, 0)),
            pl.BlockSpec((windows, LANES), lambda c: (0, c)),
            pl.BlockSpec((samples, samples), lambda c: (0, 0)),
            pl.BlockSpec((samples, samples), lambda c: (0, 0)),
        ],
        out_specs=pl.BlockSpec((half, 2 * windows, LANES), lambda c: (0, 0, c)),
        out_shape=jax.ShapeDtypeStruct((half, 2 * windows, channels), jnp.bfloat16),
        scratch_shapes=[pltpu.VMEM((half * (2 * windows + PAD), LANES), jnp.float32)],
        compiler_params=pltpu.CompilerParams(vmem_limit_bytes=32 * 2**20),
        name="whiten",
    )(picked, keep, jnp.asarray(high), jnp.asarray(low))


def pairs_kernel(place_ref, a_ref, b_ref, t_ref, *rest, nk, steps):
    o_ref, even_ref, odd_ref = rest[-3:]
    g = pl.program_id(0)
    half = a_ref.shape[1]
    windows = a_ref.shape[2] // 2
    chans = o_ref.shape[0]
    pitch = 2 * half + PAD
    rounds = half // nk
    ni = chans // rounds

    def cross(x_ref, it):
        for u in range(nk):
            k = it * nk + u
            a = a_ref[0, k]
            b = b_ref[0, k]
            turned = jnp.concatenate([-b[windows:], b[:windows]], axis=0)
            both = jnp.concatenate([b, turned], axis=1)
            y = lax.dot_general(
                a, both, (((0,), (0,)), ((), ())), preferred_element_type=jnp.float32
            )
            x_ref[pl.ds(k, chans, stride=pitch), :] = y[:, :LANES]
            x_ref[pl.ds(half + k, chans, stride=pitch), :] = y[:, LANES:]

    def lag(x_ref, it):
        for u in range(ni):
            i = it * ni + u
            start = pl.multiple_of(i * pitch, 8)
            x = x_ref[pl.ds(start, 2 * half), :].astype(jnp.bfloat16)
            y = lax.dot_general(
                x, t_ref[...], (((0,), (0,)), ((), ())), preferred_element_type=jnp.float32
            )
            o_ref[i] = y.astype(jnp.bfloat16)

    def loop(body):
        lax.fori_loop(0, rounds, lambda it, carry: (body(it), carry)[1], 0)

    def both_of(new_ref, old_ref):
        def body(it):
            lag(old_ref, it)
            cross(new_ref, it)

        loop(body)

    last = steps
    pl.when(g == 0)(lambda: loop(lambda it: cross(even_ref, it)))
    if steps > 1:
        middle = (g > 0) & (g < last)
        pl.when(middle & (g % 2 == 0))(lambda: both_of(even_ref, odd_ref))
        pl.when(middle & (g % 2 == 1))(lambda: both_of(odd_ref, even_ref))
    tail_ref = odd_ref if last % 2 == 0 else even_ref
    pl.when(g == last)(lambda: loop(lambda it: lag(tail_ref, it)))

    back = jnp.maximum(g - 1, 0)

    @pl.when((g > 0) & (place_ref[4 * back + 2] == place_ref[4 * back + 3]))
    def _():
        def clear(i, carry):
            start = pl.multiple_of(i // 16 * 16, 16)
            rows = o_ref[i, pl.ds(start, 16), :]
            ids = lax.broadcasted_iota(jnp.int32, rows.shape, 0) + start
            o_ref[i, pl.ds(start, 16), :] = jnp.where(ids == i, 0.0, rows.astype(jnp.float32)).astype(
                jnp.bfloat16
            )
            return carry

        lax.fori_loop(0, chans, clear, 0, unroll=8)


def correlate(rows, cols, table, place, shape, out):
    half = rows.shape[1]
    parts = rows.shape[2]
    table_spec = pl.BlockSpec(table.shape, lambda g, p: (0, 0))
    slots, blocks, steps = place

    def now(g):
        return jnp.minimum(g, steps - 1)

    def before(g):
        return jnp.maximum(g - 1, 0)

    nrow, ncol = shape[0] // LANES, shape[1] // LANES
    inputs = [rows, cols, table]
    in_specs = [
        pl.BlockSpec((1, half, parts, LANES), lambda g, p: (slots[0](now(g)), 0, 0, 0)),
        pl.BlockSpec((1, half, parts, LANES), lambda g, p: (slots[1](now(g)), 0, 0, 0)),
        table_spec,
    ]
    aliases = {}
    if out is not None:
        inputs.append(out)
        in_specs.append(pl.BlockSpec(memory_space=pl.ANY))
        aliases = {4: 0}
    return pl.pallas_call(
        functools.partial(pairs_kernel, nk=min(32, half), steps=steps),
        grid_spec=pltpu.PrefetchScalarGridSpec(
            num_scalar_prefetch=1,
            grid=(steps + 1,),
            in_specs=in_specs,
            out_specs=pl.BlockSpec(
                (LANES, LANES, shape[2]),
                lambda g, p: (p[4 * before(g)], p[4 * before(g) + 1], 0),
            ),
            scratch_shapes=[pltpu.VMEM((LANES * (2 * half + PAD), LANES), jnp.float32)] * 2,
        ),
        out_shape=jax.ShapeDtypeStruct(shape, jnp.bfloat16),
        input_output_aliases=aliases,
        compiler_params=pltpu.CompilerParams(vmem_limit_bytes=56 * 2**20),
        cost_estimate=pl.CostEstimate(
            flops=int((7 * steps + 5) * 1e9), bytes_accessed=steps * 2**22, transcendentals=0
        ),
        name="pairs",
    )(blocks, *inputs)


def rectangle(nr, nc, first_row, first_col, here, row, col, turn_r, turn_c):
    slots = (lambda g: g // nc, lambda g: g % nc)
    step = jnp.arange(nr * nc, dtype=jnp.int32)
    row_block = (here + first_row + step // nc) % turn_r
    col_block = (here + first_col + step % nc) % turn_c
    blocks = jnp.stack(
        [row_block, col_block, row * turn_r + row_block, col * turn_c + col_block], axis=1
    ).reshape(-1)
    return slots, blocks, nr * nc


def local(raw_traces, channel_pick, clip_mask, *, n_row, n_col):
    owned = channel_pick.shape[0]
    windows = raw_traces.shape[1]
    samples = raw_traces.shape[2]
    half = samples // 2
    row, col = lax.axis_index("row"), lax.axis_index("col")
    paired = raw_traces.reshape(owned, 2, windows, samples)
    parity = (channel_pick % 2)[:, None, None]
    picked = jnp.where(parity == 1, paired[:, 1], paired[:, 0]).transpose(1, 0, 2)
    keep = clip_mask.astype(jnp.float32).T
    table = jnp.asarray(lag_table(samples, L, windows))
    tile_r, tile_c = owned * n_col, owned * n_row
    shape = (tile_r, tile_c, L)

    if owned % LANES != 0 or n_row != n_col or n_row % 2 or n_row & (n_row - 1):
        fill = -owned % LANES
        picked = jnp.pad(picked, ((0, 0), (0, fill), (0, 0)))
        keep = jnp.pad(keep, ((0, 0), (0, fill)))
        z = whiten(picked, keep)[:, :, :owned]
        first = lax.all_gather(z, "col", axis=2, tiled=True)
        mine = jnp.where(row == col, first, 0).astype(first.dtype)
        second = lax.psum(mine, "row")

        def blocked(v):
            return v.reshape(half, 2 * windows, -1, LANES).transpose(2, 0, 1, 3)

        nr, nc = tile_r // LANES, tile_c // LANES
        place = rectangle(nr, nc, 0, 0, 0, row, col, nr, nc)
        return correlate(blocked(first), blocked(second), table, place, shape, None)

    z = whiten(picked, keep)
    n = n_col
    ring = [(j, (j - 1) % n) for j in range(n)]
    per = owned // LANES

    def share(v):
        held = {c: {c} for c in range(n_col)}
        bit = n_row // 2
        while bit:
            moves = [(r * n_col + c, (r ^ bit) * n_col + c) for c in range(n_col) for r in sorted(held[c])]
            got = lax.ppermute(v, ("row", "col"), moves)
            mask = ~(2 * bit - 1)
            keeps = ((row ^ col) & bit) == 0
            v = jnp.where(keeps, v, got)
            for c in range(n_col):
                held[c] |= {r ^ bit for r in held[c]}
            bit //= 2
        return v

    def split(v):
        return v.reshape(half, 2 * windows, per, LANES).transpose(2, 0, 1, 3)

    rows = [split(z)]
    for _ in range(n - 1):
        rows.append(lax.ppermute(rows[-1], "col", ring))
    cols = [share(v) for v in rows]
    out = None
    chunk = 2
    row_groups = [jnp.concatenate(rows[s : s + chunk]) for s in range(0, n, chunk)]
    col_groups = [jnp.concatenate(cols[s : s + chunk]) for s in range(0, n, chunk)]
    for late in range(len(row_groups)):
        for r, c in [(late, q) for q in range(late)] + [(q, late) for q in range(late + 1)]:
            place = rectangle(
                chunk * per, chunk * per, r * chunk * per, c * chunk * per, col * per, row, col, n * per, n * per
            )
            out = correlate(row_groups[r], col_groups[c], table, place, shape, out)
    return out


def solution(mesh):
    return jax.shard_map(
        functools.partial(local, n_row=mesh.shape["row"], n_col=mesh.shape["col"]),
        mesh=mesh,
        in_specs=(
            P(("seg", "row", "col"), None, None),
            P(("seg", "row", "col")),
            P(("seg", "row", "col"), None),
        ),
        out_specs=P(("seg", "row"), "col", None),
        check_vma=False,
    )
```

time: 1070 us -> 225 us (0.21)
  matrix products: 553 us -> 0 us
  local copies, waits for them, and re-layouts: 271 us -> 4.3 us
  Pallas kernels: 0 us -> 122 us
  waiting for transfers between devices: 166 us -> 48.8 us
  other arithmetic: 63.3 us -> 13.7 us
  starting transfers between devices: 0.22 us -> 36 us
  between operations: 13.5 us -> 0.19 us
    dot_general x6 -> x0, matrix products: 553 us -> none  [the longest x1 228 us: local(): jnp.dot(cross_im.reshape(-1, half), sin_table, precision=lax.Precision.HI...]
    transpose x2 -> x0, local copies, waits for them, and re-layouts: 268 us -> none  [the longest x1 134 us: local(): jnp.einsum('iwpk,jwpk->ijk', row_four, rot_four, preferred_element_type=j...]
    pallas_call x0 -> x5, Pallas kernels: none -> 122 us  [the longest x4 119 us: correlate(): pl.pallas_call(functools.partial(pairs_kernel, nk=min(32, half), steps=st...]
    all_gather x1 -> x0, waiting for transfers between devices: 83.2 us -> none  [local(): lax.all_gather(outgoing, 'col', axis=0, tiled=True)]
    psum x1 -> x0, waiting for transfers between devices: 82.9 us -> none  [broadcast(): return lax.psum(kept, axis)]
    convert_element_type x2 -> x0, other arithmetic: 49.9 us -> none  [the longest x1 49.9 us: local(): return jnp.where(same[:, :, None], 0.0, lagged).astype(jnp.bfloat16)]
    ppermute x0 -> x11, waiting for transfers between devices: none -> 48.8 us  [the longest x3 47 us: local(): rows.append(lax.ppermute(rows[-1], 'col', ring))]
    ppermute x0 -> x11, starting transfers between devices: none -> 36 us  [the longest x8 26 us: share(): got = lax.ppermute(v, ('row', 'col'), moves)]
  transfers between devices with their start and end apart: 2 -> 11, of which waited for: 2 -> 4; matrix products, arithmetic and copies ran while one was open for 0% -> 5% of each run, Pallas kernels for 0% -> 26%
where the time goes in v1:
time: 225 us
  Pallas kernels  122 us (54%)
  waiting for transfers between devices  48.8 us (22%)
  starting transfers between devices  36 us (16%)
  other arithmetic  13.7 us (6%)
  local copies, waits for them, and re-layouts  4.3 us (2%)
    pallas_call x4, Pallas kernels, correlate(): pl.pallas_call(functools.partial(pairs_kernel, nk=min(32, half), steps=st...  119 us
    ppermute x3, waiting for transfers between devices, local(): rows.append(lax.ppermute(rows[-1], 'col', ring))  47 us
    ppermute x8, starting transfers between devices, share(): got = lax.ppermute(v, ('row', 'col'), moves)  26 us
    ppermute x3, starting transfers between devices, local(): rows.append(lax.ppermute(rows[-1], 'col', ring))  10 us
    select_n x8, other arithmetic, share(): v = jnp.where(keeps, v, got)  5.24 us
  transfers between devices with their start and end apart: 11, of which 4 were waited for; matrix products, arithmetic and copies ran while one was open for 5% of the time, Pallas kernels for 26%

profile of v1, /device:TPU:0, one launch (start us, length us, event | category | flops | bytes accessed | tf_op | source)
XLA Modules:
  0.0 224.8 jit_solution(3631384192900292180)
XLA Ops:
  0.0 0.7 fusion.15
  0.7 0.7 convert_bitcast_fusion.keep_ref
  1.4 1.7 fusion.17
  3.1 0.0 copy-start
  3.1 0.0 copy-start.1
  3.1 1.2 fusion.1.raw_ref
  4.3 2.9 %whiten.1 = bf16[128,32,128]{2,1,0:T(8,128)(2,1)S(1)} custom-call(bf16[16,128,256]{2,1,0:T(8,128)(2,1)S(1)} %fusion.1.raw_ref, f32[16,128]{1,0:T(8,128)S(1)} %convert_bitcast_fusion.keep_ref, bf16[256,256]{1,0:T(8,128)(2,1)S(1)} %copy-done.1, bf16[256,256]{1,0:T(8,128)(2,1)S(1)} %copy-done), custom_call_target="tpu_custom_call" | custom-call | tf_op jit(solution)/shard_map/whiten/pallas_call | solution.py:78
  7.1 5.1 %collective-permute-start = (bf16[1,128,32,128]{3,2,1,0:T(8,128)(2,1)S(1)}, bf16[1,128,32,128]{3,2,1,0:T(8,128)(2,1)S(1)}, u32[]{:S(2)}, u32[]{:S(2)}) collective-permute-start(bf16[1,128,32,128]{3,2,1,0:T(8,128)(2,1)S(1)} %bitcast.17), channel_id=1, source_target_pairs={{0,3},{1,0},{2,1},{3,2},{4,7},{5,4},{6,5},{7,6},{8,11},{9,8},{10,9... | collective-permute-start | bytes 3145736 | tf_op jit(solution)/shard_map/ppermute | solution.py:274
  12.2 4.4 %collective-permute-start.7 = (bf16[1,128,32,128]{3,2,1,0:T(8,128)(2,1)S(1)}, bf16[1,128,32,128]{3,2,1,0:T(8,128)(2,1)}, u32[]{:S(2)}, u32[]{:S(2)}) collective-permute-start(bf16[1,128,32,128]{3,2,1,0:T(8,128)(2,1)S(1)} %bitcast.18), channel_id=1, source_target_pairs={{0,8},{5,13},{10,2},{15,7},{16,24},{21,29},{26,18},{31,23}} | collective-permute-start | bytes 3145736 | tf_op jit(solution)/shard_map/ppermute | solution.py:260
  16.6 18.1 %collective-permute-done = bf16[1,128,32,128]{3,2,1,0:T(8,128)(2,1)S(1)} collective-permute-done((bf16[1,128,32,128]{3,2,1,0:T(8,128)(2,1)S(1)}, bf16[1,128,32,128]{3,2,1,0:T(8,128)(2,1)S(1)}, u32[]{:S(2)}, u32[]{:S(2)}) %collective-permute-start) | collective-permute-done | bytes 1048608 | tf_op jit(solution)/shard_map/ppermute | solution.py:274
  34.7 4.3 %collective-permute-start.1 = (bf16[1,128,32,128]{3,2,1,0:T(8,128)(2,1)S(1)}, bf16[1,128,32,128]{3,2,1,0:T(8,128)(2,1)}, u32[]{:S(2)}, u32[]{:S(2)}) collective-permute-start(bf16[1,128,32,128]{3,2,1,0:T(8,128)(2,1)S(1)} %collective-permute-done), channel_id=1, source_target_pairs={{0,3},{1,0},{2,1},{3,2},{4,7},{5,4},{6,5},{7,6},{8,11},{9,8},{10,9... | collective-permute-start | bytes 3145736 | tf_op jit(solution)/shard_map/ppermute | solution.py:274
  38.9 4.4 %collective-permute-start.9 = (bf16[1,128,32,128]{3,2,1,0:T(8,128)(2,1)S(1)}, bf16[1,128,32,128]{3,2,1,0:T(8,128)(2,1)}, u32[]{:S(2)}, u32[]{:S(2)}) collective-permute-start(bf16[1,128,32,128]{3,2,1,0:T(8,128)(2,1)S(1)} %collective-permute-done), channel_id=1, source_target_pairs={{0,8},{5,13},{10,2},{15,7},{16,24},{21,29},{26,18},{31,23}} | collective-permute-start | bytes 3145736 | tf_op jit(solution)/shard_map/ppermute | solution.py:260
  43.3 0.0 collective-permute-done.7
  43.3 0.1 broadcast_select_fusion.1
  43.5 2.3 %collective-permute-start.8 = (bf16[1,128,32,128]{3,2,1,0:T(8,128)(2,1)S(1)}, bf16[1,128,32,128]{3,2,1,0:T(8,128)(2,1)}, u32[]{:S(2)}, u32[]{:S(2)}) collective-permute-start(bf16[1,128,32,128]{3,2,1,0:T(8,128)(2,1)S(1)} %broadcast_select_fusion.1), channel_id=1, source_target_pairs={{0,4},{8,12},{5,1},{13,9},{2,6},{10,14},{7,3},{15,11},{16,20},{24,... | collective-permute-start | bytes 3145736 | tf_op jit(solution)/shard_map/ppermute | solution.py:260
  45.8 14.7 %collective-permute-done.1 = bf16[1,128,32,128]{3,2,1,0:T(8,128)(2,1)} collective-permute-done((bf16[1,128,32,128]{3,2,1,0:T(8,128)(2,1)S(1)}, bf16[1,128,32,128]{3,2,1,0:T(8,128)(2,1)}, u32[]{:S(2)}, u32[]{:S(2)}) %collective-permute-start.1) | collective-permute-done | bytes 1048608 | tf_op jit(solution)/shard_map/ppermute | solution.py:274
  60.5 4.4 %collective-permute-start.3 = (bf16[1,128,32,128]{3,2,1,0:T(8,128)(2,1)}, bf16[1,128,32,128]{3,2,1,0:T(8,128)(2,1)}, u32[]{:S(2)}, u32[]{:S(2)}) collective-permute-start(bf16[1,128,32,128]{3,2,1,0:T(8,128)(2,1)} %collective-permute-done.1), channel_id=1, source_target_pairs={{0,8},{5,13},{10,2},{15,7},{16,24},{21,29},{26,18},{31,23}} | collective-permute-start | bytes 3145736 | tf_op jit(solution)/shard_map/ppermute | solution.py:260
  64.9 0.0 collective-permute-done.9
  64.9 1.3 broadcast_select_fusion
  66.2 2.3 %collective-permute-start.10 = (bf16[1,128,32,128]{3,2,1,0:T(8,128)(2,1)S(1)}, bf16[1,128,32,128]{3,2,1,0:T(8,128)(2,1)}, u32[]{:S(2)}, u32[]{:S(2)}) collective-permute-start(bf16[1,128,32,128]{3,2,1,0:T(8,128)(2,1)S(1)} %broadcast_select_fusion), channel_id=1, source_target_pairs={{0,4},{8,12},{5,1},{13,9},{2,6},{10,14},{7,3},{15,11},{16,20},{24,... | collective-permute-start | bytes 3145736 | tf_op jit(solution)/shard_map/ppermute | solution.py:260
  68.6 0.1 add_add_fusion.3
  68.6 0.6 reshape.233.place_ref
  69.3 0.6 reshape.232.place_ref
  69.9 0.7 reshape.229.place_ref
  70.5 0.7 reshape.231.place_ref
  71.2 2.7 %pad_maximum_fusion.1.a_ref = bf16[2,128,32,128]{3,2,1,0:T(8,128)(2,1)} fusion(bf16[1,128,32,128]{3,2,1,0:T(8,128)(2,1)} %copy-done.3, bf16[1,128,32,128]{3,2,1,0:T(8,128)(2,1)S(1)} %bitcast.19), kind=kLoop, calls=%fused_computation.1 | loop fusion | flops 1048576 | bytes 4194304 | tf_op jit(solution)/shard_map/concatenate | solution.py:278
  74.0 0.7 collective-permute-start.2
  74.6 0.0 collective-permute-done.8
  74.6 0.1 broadcast_select_fusion.5
  74.7 1.8 collective-permute-done.3
  76.5 1.6 broadcast_select_fusion.3
  78.1 3.3 %collective-permute-start.4 = (bf16[1,128,32,128]{3,2,1,0:T(8,128)(2,1)S(1)}, bf16[1,128,32,128]{3,2,1,0:T(8,128)(2,1)S(1)}, u32[]{:S(2)}, u32[]{:S(2)}) collective-permute-start(bf16[1,128,32,128]{3,2,1,0:T(8,128)(2,1)S(1)} %get-tuple-element.7), channel_id=1, source_target_pairs={{0,4},{8,12},{5,1},{13,9},{2,6},{10,14},{7,3},{15,11},{16,20},{24,... | collective-permute-start | bytes 3145736 | tf_op jit(solution)/shard_map/ppermute | solution.py:260
  81.4 0.0 collective-permute-done.10
  81.4 0.1 broadcast_select_fusion.4
  81.6 1.5 pad_maximum_fusion.2.b_ref
  83.1 14.2 %collective-permute-done.2 = bf16[1,128,32,128]{3,2,1,0:T(8,128)(2,1)} collective-permute-done((bf16[1,128,32,128]{3,2,1,0:T(8,128)(2,1)}, bf16[1,128,32,128]{3,2,1,0:T(8,128)(2,1)}, u32[]{:S(2)}, u32[]{:S(2)}) %collective-permute-start.2) | collective-permute-done | bytes 1048608 | tf_op jit(solution)/shard_map/ppermute | solution.py:274
  97.3 3.4 %collective-permute-start.5 = (bf16[1,128,32,128]{3,2,1,0:T(8,128)(2,1)}, bf16[1,128,32,128]{3,2,1,0:T(8,128)(2,1)S(1)}, u32[]{:S(2)}, u32[]{:S(2)}) collective-permute-start(bf16[1,128,32,128]{3,2,1,0:T(8,128)(2,1)} %collective-permute-done.2), channel_id=1, source_target_pairs={{0,8},{5,13},{10,2},{15,7},{16,24},{21,29},{26,18},{31,23}} | collective-permute-start | bytes 3145736 | tf_op jit(solution)/shard_map/ppermute | solution.py:260
  100.8 30.6 %pairs.4.rest_0_ = bf16[512,512,128]{2,1,0:T(8,128)(2,1)} custom-call(s32[16]{0:T(128)} %reshape.233.place_ref, bf16[2,128,32,128]{3,2,1,0:T(8,128)(2,1)} %pad_maximum_fusion.1.a_ref, bf16[2,128,32,128]{3,2,1,0:T(8,128)(2,1)} %pad_maximum_fusion.2.b_ref, bf16[256,128]{1,0:T(8,128)(2,1)} %constant.112.clone.t_ref), custom_call_target="tpu_custom_call" | custom-call | flops 32999999488 | bytes 16777216 | tf_op jit(solution)/shard_map/pairs/pallas_call | solution.py:187
  131.3 0.0 collective-permute-done.5
  131.3 1.7 broadcast_select_fusion.2
  133.0 1.5 collective-permute-start.6
  134.6 28.8 %pairs.5.rest_0_ = bf16[512,512,128]{2,1,0:T(8,128)(2,1)} custom-call(s32[16]{0:T(128)} %reshape.232.place_ref, bf16[2,128,32,128]{3,2,1,0:T(8,128)(2,1)} %copy-done.2, bf16[2,128,32,128]{3,2,1,0:T(8,128)(2,1)} %pad_maximum_fusion.2.b_ref, bf16[256,128]{1,0:T(8,128)(2,1)} %constant.112.clone.t_ref, ...), custom_call_target="tpu_custom_call", output_to_operand_aliasing={{}: (4, {})} | custom-call | flops 32999999488 | bytes 16777216 | tf_op jit(solution)/shard_map/pairs/pallas_call | solution.py:187
  163.4 0.1 broadcast_select_fusion.7
  163.5 0.0 collective-permute-done.6
  163.5 0.1 broadcast_select_fusion.6
  163.7 1.5 pad_maximum_fusion.b_ref
  165.2 28.8 %pairs.6.rest_0_ = bf16[512,512,128]{2,1,0:T(8,128)(2,1)} custom-call(s32[16]{0:T(128)} %reshape.231.place_ref, bf16[2,128,32,128]{3,2,1,0:T(8,128)(2,1)} %pad_maximum_fusion.1.a_ref, bf16[2,128,32,128]{3,2,1,0:T(8,128)(2,1)} %pad_maximum_fusion.b_ref, bf16[256,128]{1,0:T(8,128)(2,1)} %constant.112.clone.t_ref, ...), custom_call_target="tpu_custom_call", output_to_operand_aliasing={{}: (4, {})} | custom-call | flops 32999999488 | bytes 16777216 | tf_op jit(solution)/shard_map/pairs/pallas_call | solution.py:187
  194.0 30.8 %pairs.7 = bf16[512,512,128]{2,1,0:T(8,128)(2,1)} custom-call(s32[16]{0:T(128)} %reshape.229.place_ref, bf16[2,128,32,128]{3,2,1,0:T(8,128)(2,1)} %copy-done.2, bf16[2,128,32,128]{3,2,1,0:T(8,128)(2,1)} %pad_maximum_fusion.b_ref, bf16[256,128]{1,0:T(8,128)(2,1)} %constant.112.clone.t_ref, ...), custom_call_target="tpu_custom_call", output_to_operand_aliasing={{}: (4, {})} | custom-call | flops 32999999488 | bytes 16777216 | tf_op jit(solution)/shard_map/pairs/pallas_call | solution.py:187
  (11 shorter events, 0.1 us)
Async XLA Ops:
  3.1 1.2 copy-start
  3.1 1.2 copy-start.1
  7.1 27.5 %collective-permute-start = (bf16[1,128,32,128]{3,2,1,0:T(8,128)(2,1)S(1)}, bf16[1,128,32,128]{3,2,1,0:T(8,128)(2,1)S(1)}, u32[]{:S(2)}, u32[]{:S(2)}) collective-permute-start(bf16[1,128,32,128]{3,2,1,0:T(8,128)(2,1)S(1)} %bitcast.17), channel_id=1, source_target_pairs={{0,3},{1,0},{2,1},{3,2},{4,7},{5,4},{6,5},{7,6},{8,11},{9,8},{10,9... | collective-permute-start | bytes 3145736 | tf_op jit(solution)/shard_map/ppermute | solution.py:274
  12.2 31.1 %collective-permute-start.7 = (bf16[1,128,32,128]{3,2,1,0:T(8,128)(2,1)S(1)}, bf16[1,128,32,128]{3,2,1,0:T(8,128)(2,1)}, u32[]{:S(2)}, u32[]{:S(2)}) collective-permute-start(bf16[1,128,32,128]{3,2,1,0:T(8,128)(2,1)S(1)} %bitcast.18), channel_id=1, source_target_pairs={{0,8},{5,13},{10,2},{15,7},{16,24},{21,29},{26,18},{31,23}} | collective-permute-start | bytes 3145736 | tf_op jit(solution)/shard_map/ppermute | solution.py:260
  34.7 30.2 %copy-start.3 = (bf16[1,128,32,128]{3,2,1,0:T(8,128)(2,1)}, bf16[1,128,32,128]{3,2,1,0:T(8,128)(2,1)S(1)}, u32[]{:S(2)}) copy-start(bf16[1,128,32,128]{3,2,1,0:T(8,128)(2,1)S(1)} %collective-permute-done) | copy-start | bytes 3145732
  34.7 25.8 %collective-permute-start.1 = (bf16[1,128,32,128]{3,2,1,0:T(8,128)(2,1)S(1)}, bf16[1,128,32,128]{3,2,1,0:T(8,128)(2,1)}, u32[]{:S(2)}, u32[]{:S(2)}) collective-permute-start(bf16[1,128,32,128]{3,2,1,0:T(8,128)(2,1)S(1)} %collective-permute-done), channel_id=1, source_target_pairs={{0,3},{1,0},{2,1},{3,2},{4,7},{5,4},{6,5},{7,6},{8,11},{9,8},{10,9... | collective-permute-start | bytes 3145736 | tf_op jit(solution)/shard_map/ppermute | solution.py:274
  38.9 25.9 %collective-permute-start.9 = (bf16[1,128,32,128]{3,2,1,0:T(8,128)(2,1)S(1)}, bf16[1,128,32,128]{3,2,1,0:T(8,128)(2,1)}, u32[]{:S(2)}, u32[]{:S(2)}) collective-permute-start(bf16[1,128,32,128]{3,2,1,0:T(8,128)(2,1)S(1)} %collective-permute-done), channel_id=1, source_target_pairs={{0,8},{5,13},{10,2},{15,7},{16,24},{21,29},{26,18},{31,23}} | collective-permute-start | bytes 3145736 | tf_op jit(solution)/shard_map/ppermute | solution.py:260
  43.5 31.2 %collective-permute-start.8 = (bf16[1,128,32,128]{3,2,1,0:T(8,128)(2,1)S(1)}, bf16[1,128,32,128]{3,2,1,0:T(8,128)(2,1)}, u32[]{:S(2)}, u32[]{:S(2)}) collective-permute-start(bf16[1,128,32,128]{3,2,1,0:T(8,128)(2,1)S(1)} %broadcast_select_fusion.1), channel_id=1, source_target_pairs={{0,4},{8,12},{5,1},{13,9},{2,6},{10,14},{7,3},{15,11},{16,20},{24,... | collective-permute-start | bytes 3145736 | tf_op jit(solution)/shard_map/ppermute | solution.py:260
  60.5 16.0 %collective-permute-start.3 = (bf16[1,128,32,128]{3,2,1,0:T(8,128)(2,1)}, bf16[1,128,32,128]{3,2,1,0:T(8,128)(2,1)}, u32[]{:S(2)}, u32[]{:S(2)}) collective-permute-start(bf16[1,128,32,128]{3,2,1,0:T(8,128)(2,1)} %collective-permute-done.1), channel_id=1, source_target_pairs={{0,8},{5,13},{10,2},{15,7},{16,24},{21,29},{26,18},{31,23}} | collective-permute-start | bytes 3145736 | tf_op jit(solution)/shard_map/ppermute | solution.py:260
  66.2 15.2 %collective-permute-start.10 = (bf16[1,128,32,128]{3,2,1,0:T(8,128)(2,1)S(1)}, bf16[1,128,32,128]{3,2,1,0:T(8,128)(2,1)}, u32[]{:S(2)}, u32[]{:S(2)}) collective-permute-start(bf16[1,128,32,128]{3,2,1,0:T(8,128)(2,1)S(1)} %broadcast_select_fusion), channel_id=1, source_target_pairs={{0,4},{8,12},{5,1},{13,9},{2,6},{10,14},{7,3},{15,11},{16,20},{24,... | collective-permute-start | bytes 3145736 | tf_op jit(solution)/shard_map/ppermute | solution.py:260
  74.0 23.4 %collective-permute-start.2 = (bf16[1,128,32,128]{3,2,1,0:T(8,128)(2,1)}, bf16[1,128,32,128]{3,2,1,0:T(8,128)(2,1)}, u32[]{:S(2)}, u32[]{:S(2)}) collective-permute-start(bf16[1,128,32,128]{3,2,1,0:T(8,128)(2,1)} %collective-permute-done.1), channel_id=1, source_target_pairs={{0,3},{1,0},{2,1},{3,2},{4,7},{5,4},{6,5},{7,6},{8,11},{9,8},{10,9... | collective-permute-start | bytes 3145736 | tf_op jit(solution)/shard_map/ppermute | solution.py:274
  78.1 85.3 %collective-permute-start.4 = (bf16[1,128,32,128]{3,2,1,0:T(8,128)(2,1)S(1)}, bf16[1,128,32,128]{3,2,1,0:T(8,128)(2,1)S(1)}, u32[]{:S(2)}, u32[]{:S(2)}) collective-permute-start(bf16[1,128,32,128]{3,2,1,0:T(8,128)(2,1)S(1)} %get-tuple-element.7), channel_id=1, source_target_pairs={{0,4},{8,12},{5,1},{13,9},{2,6},{10,14},{7,3},{15,11},{16,20},{24,... | collective-permute-start | bytes 3145736 | tf_op jit(solution)/shard_map/ppermute | solution.py:260
  97.3 34.0 %collective-permute-start.5 = (bf16[1,128,32,128]{3,2,1,0:T(8,128)(2,1)}, bf16[1,128,32,128]{3,2,1,0:T(8,128)(2,1)S(1)}, u32[]{:S(2)}, u32[]{:S(2)}) collective-permute-start(bf16[1,128,32,128]{3,2,1,0:T(8,128)(2,1)} %collective-permute-done.2), channel_id=1, source_target_pairs={{0,8},{5,13},{10,2},{15,7},{16,24},{21,29},{26,18},{31,23}} | collective-permute-start | bytes 3145736 | tf_op jit(solution)/shard_map/ppermute | solution.py:260
  133.0 1.6 copy-start.2
  133.0 30.5 %collective-permute-start.6 = (bf16[1,128,32,128]{3,2,1,0:T(8,128)(2,1)S(1)}, bf16[1,128,32,128]{3,2,1,0:T(8,128)(2,1)S(1)}, u32[]{:S(2)}, u32[]{:S(2)}) collective-permute-start(bf16[1,128,32,128]{3,2,1,0:T(8,128)(2,1)S(1)} %get-tuple-element.9), channel_id=1, source_target_pairs={{0,4},{8,12},{5,1},{13,9},{2,6},{10,14},{7,3},{15,11},{16,20},{24,... | collective-permute-start | bytes 3145736 | tf_op jit(solution)/shard_map/ppermute | solution.py:260

commit v2 on v1

v2 whole, which is shorter than its diff:
```python
import functools
import math

import jax
import jax.numpy as jnp
import ml_dtypes
import numpy as np
from jax import lax
from jax.experimental import pallas as pl
from jax.experimental.pallas import tpu as pltpu
from jax.sharding import PartitionSpec as P

L = 128
LANES = 128
PAD = 8


def spectrum_tables(samples):
    half = samples // 2
    freq = np.arange(1, half + 1)
    pos = np.arange(samples)
    angle = (freq[:, None] * pos[None, :] % samples) * (2.0 * np.pi / samples)
    table = np.concatenate([np.cos(angle), -np.sin(angle)], axis=0).astype(np.float32)
    high = table.astype(ml_dtypes.bfloat16)
    low = (table - high.astype(np.float32)).astype(ml_dtypes.bfloat16)
    return np.stack([high, low])


def lag_table(samples, lags, windows):
    half = samples // 2
    freq = np.arange(1, half + 1)
    shift = np.arange(lags) - lags // 2
    angle = (freq[:, None] * shift[None, :] % samples) * (2.0 * np.pi / samples)
    scale = 1.0 / math.sqrt(windows * half)
    table = np.concatenate([np.cos(angle), -np.sin(angle)], axis=0) * scale
    return table.T.astype(ml_dtypes.bfloat16)


def whiten_kernel(raw_ref, keep_ref, table_ref, z_ref, rows_ref):
    windows = raw_ref.shape[0]
    half = table_ref.shape[1] // 2
    parts = 2 * windows
    pitch = parts + PAD
    contract = (((1,), (1,)), ((), ()))

    def window(w, carry):
        raw = raw_ref[w]
        spec = lax.dot_general(table_ref[0], raw, contract, preferred_element_type=jnp.float32)
        spec += lax.dot_general(table_ref[1], raw, contract, preferred_element_type=jnp.float32)
        real, imag = spec[:half], spec[half:]
        power = real * real + imag * imag
        total = power
        for gap in (1, 2):
            edge = jnp.zeros((gap, power.shape[1]), jnp.float32)
            total += jnp.concatenate([power[gap:], edge], axis=0)
            total += jnp.concatenate([edge, power[:-gap]], axis=0)
        mean = jnp.sum(power, axis=0, keepdims=True) * (1.0 / half)
        denom = jnp.sqrt(total * 0.2 + 0.1 * mean + 1e-06)
        weight = keep_ref[pl.ds(w, 1), :] / denom
        rows_ref[pl.ds(w, half, stride=pitch), :] = real * weight
        rows_ref[pl.ds(windows + w, half, stride=pitch), :] = imag * weight
        return carry

    lax.fori_loop(0, windows, window, 0, unroll=4)

    def narrow(k, carry):
        start = pl.multiple_of(k * pitch, 8)
        z_ref[k] = rows_ref[pl.ds(start, parts), :].astype(jnp.bfloat16)
        return carry

    lax.fori_loop(0, half, narrow, 0, unroll=8)


def whiten(picked, keep):
    windows, channels, samples = picked.shape
    half = samples // 2
    return pl.pallas_call(
        whiten_kernel,
        grid=(channels // LANES,),
        in_specs=[
            pl.BlockSpec((windows, LANES, samples), lambda c: (0, c, 0)),
            pl.BlockSpec((windows, LANES), lambda c: (0, c)),
            pl.BlockSpec((2, samples, samples), lambda c: (0, 0, 0)),
        ],
        out_specs=pl.BlockSpec((half, 2 * windows, LANES), lambda c: (0, 0, c)),
        out_shape=jax.ShapeDtypeStruct((half, 2 * windows, channels), jnp.bfloat16),
        scratch_shapes=[pltpu.VMEM((half * (2 * windows + PAD), LANES), jnp.float32)],
        compiler_params=pltpu.CompilerParams(vmem_limit_bytes=32 * 2**20),
        name="whiten",
    )(picked, keep, jnp.asarray(spectrum_tables(samples)))


def pairs_kernel(slots_ref, here_ref, *refs, pairs, nr, routes, nk, turn):
    rows, cols = refs[:nr], []
    at = nr
    for route in routes:
        cols.append(list(zip(refs[at : at + len(route)], route, strict=True)))
        at += len(route)
    t_ref = refs[at]
    o_ref, even_ref, odd_ref, a_ref, b_ref, a_sem, b_sem = refs[-7:]
    g = pl.program_id(0)
    last = len(pairs)
    half = a_ref.shape[1]
    windows = a_ref.shape[2] // 2
    chans = o_ref.shape[0]
    pitch = 2 * half + PAD
    rounds = half // nk
    ni = chans // rounds

    def row_copy(step):
        slot = step % 2
        return pltpu.make_async_copy(rows[pairs[step][0]], a_ref.at[slot], a_sem.at[slot])

    def col_copy(step, ref):
        slot = step % 2
        return pltpu.make_async_copy(ref, b_ref.at[slot], b_sem.at[slot])

    def start(step):
        row_copy(step).start()
        for ref, ways in cols[pairs[step][1]]:
            here = functools.reduce(jnp.logical_or, [here_ref[3] == way for way in ways])
            pl.when(here)(lambda: col_copy(step, ref).start())

    pl.when(g == 0)(lambda: start(0))
    for step in range(last):

        @pl.when(g == step)
        def _():
            if step + 1 < last:
                start(step + 1)
            row_copy(step).wait()
            col_copy(step, cols[pairs[step][1]][0][0]).wait()

    def cross(x_ref, it, slot):
        for u in range(nk):
            k = it * nk + u
            a = a_ref[slot, k]
            b = b_ref[slot, k]
            turned = jnp.concatenate([-b[windows:], b[:windows]], axis=0)
            both = jnp.concatenate([b, turned], axis=1)
            y = lax.dot_general(
                a, both, (((0,), (0,)), ((), ())), preferred_element_type=jnp.float32
            )
            x_ref[pl.ds(k, chans, stride=pitch), :] = y[:, :LANES]
            x_ref[pl.ds(half + k, chans, stride=pitch), :] = y[:, LANES:]

    def slab(x_ref, i):
        start = pl.multiple_of(i * pitch, 8)
        return x_ref[pl.ds(start, 2 * half), :].astype(jnp.bfloat16)

    def lag(x_ref, it):
        for u in range(0, ni, 2):
            i = it * ni + u
            x = jnp.concatenate([slab(x_ref, i), slab(x_ref, i + 1)], axis=1)
            y = jnp.dot(t_ref[...], x, preferred_element_type=jnp.float32).astype(jnp.bfloat16)
            o_ref[i] = y[:, :LANES].T
            o_ref[i + 1] = y[:, LANES:].T

    def loop(body):
        lax.fori_loop(0, rounds, lambda it, carry: (body(it), carry)[1], 0)

    def both_of(new_ref, old_ref, slot):
        def body(it):
            lag(old_ref, it)
            cross(new_ref, it, slot)

        loop(body)

    pl.when(g == 0)(lambda: loop(lambda it: cross(even_ref, it, 0)))
    if last > 1:
        middle = (g > 0) & (g < last)
        pl.when(middle & (g % 2 == 1))(lambda: both_of(odd_ref, even_ref, 1))
    if last > 2:
        pl.when(middle & (g % 2 == 0))(lambda: both_of(even_ref, odd_ref, 0))
    tail_ref = odd_ref if last % 2 == 0 else even_ref
    pl.when(g == last)(lambda: loop(lambda it: lag(tail_ref, it)))

    back = jnp.maximum(g - 1, 0)

    block_r, block_c = block_at(back, slots_ref, here_ref, turn)
    first_r, first_c = here_ref[0] * turn[0], here_ref[1] * turn[1]

    @pl.when((g > 0) & (first_r + block_r == first_c + block_c))
    def _():
        def clear(i, carry):
            start = pl.multiple_of(i // 16 * 16, 16)
            rows = o_ref[i, pl.ds(start, 16), :]
            ids = lax.broadcasted_iota(jnp.int32, rows.shape, 0) + start
            kept = jnp.where(ids == i, 0.0, rows.astype(jnp.float32))
            o_ref[i, pl.ds(start, 16), :] = kept.astype(jnp.bfloat16)
            return carry

        lax.fori_loop(0, chans, clear, 0, unroll=8)


def block_at(step, slots_ref, here_ref, turn):
    block_r = lax.rem(slots_ref[2 * step] + here_ref[2], turn[0])
    block_c = lax.rem(slots_ref[2 * step + 1] + here_ref[2], turn[1])
    return block_r, block_c


def correlate(rows, cols, pairs, table, here, shape, out):
    half, parts = rows[0].shape[:2]
    turn = (shape[0] // LANES, shape[1] // LANES)
    slots = jnp.asarray(np.array(pairs, np.int32).reshape(-1))

    def before(g):
        return jnp.maximum(g - 1, 0)

    used_r, used_c = sorted({r for r, _ in pairs}), sorted({c for _, c in pairs})
    pairs = [(used_r.index(r), used_c.index(c)) for r, c in pairs]
    whole = pl.BlockSpec(memory_space=pl.ANY)
    inputs = [rows[r] for r in used_r] + [v for c in used_c for v, _ in cols[c]]
    routes = [[ways for _, ways in cols[c]] for c in used_c]
    in_specs = [whole] * len(inputs) + [pl.BlockSpec(table.shape, lambda g, p, q: (0, 0))]
    inputs.append(table)
    aliases = {}
    if out is not None:
        aliases = {len(inputs) + 2: 0}
        inputs.append(out)
        in_specs.append(whole)
    steps = len(pairs)
    buffer = pltpu.VMEM((2, half, parts, LANES), jnp.bfloat16)
    return pl.pallas_call(
        functools.partial(
            pairs_kernel, pairs=pairs, nr=len(used_r), routes=routes, nk=half, turn=turn
        ),
        grid_spec=pltpu.PrefetchScalarGridSpec(
            num_scalar_prefetch=2,
            grid=(steps + 1,),
            in_specs=in_specs,
            out_specs=pl.BlockSpec(
                (LANES, LANES, shape[2]),
                lambda g, p, q: (*block_at(before(g), p, q, turn), 0),
            ),
            scratch_shapes=[pltpu.VMEM((LANES * (2 * half + PAD), LANES), jnp.float32)] * 2
            + [buffer, buffer, pltpu.SemaphoreType.DMA((2,)), pltpu.SemaphoreType.DMA((2,))],
        ),
        out_shape=jax.ShapeDtypeStruct(shape, jnp.bfloat16),
        input_output_aliases=aliases,
        compiler_params=pltpu.CompilerParams(vmem_limit_bytes=56 * 2**20),
        cost_estimate=pl.CostEstimate(
            flops=int((7 * steps + 5) * 1e9), bytes_accessed=steps * 2**22, transcendentals=0
        ),
        name="pairs",
    )(slots, here, *inputs)


def hop(v, bit, held, n_col):
    moves = [(r * n_col + c, (r ^ bit) * n_col + c) for c in range(n_col) for r in sorted(held[c])]
    for kept in held:
        kept |= {r ^ bit for r in kept}
    return lax.ppermute(v, ("row", "col"), moves)


def send(v, n_row, n_col):
    return [
        lax.ppermute(v, ("row", "col"), [(c * n_col + c, (c ^ d) * n_col + c) for c in range(n_col)])
        for d in range(1, n_row)
    ]


def gate(v, after):
    return lax.optimization_barrier((v, after))[0]


def local(raw_traces, channel_pick, clip_mask, *, n_row, n_col):
    owned = channel_pick.shape[0]
    windows = raw_traces.shape[1]
    samples = raw_traces.shape[2]
    half = samples // 2
    row, col = lax.axis_index("row"), lax.axis_index("col")
    paired = raw_traces.reshape(owned, 2, windows, samples)
    parity = (channel_pick % 2)[:, None, None]
    picked = jnp.where(parity == 1, paired[:, 1], paired[:, 0]).transpose(1, 0, 2)
    keep = clip_mask.astype(jnp.float32).T
    table = jnp.asarray(lag_table(samples, L, windows))
    tile_r, tile_c = owned * n_col, owned * n_row
    shape = (tile_r, tile_c, L)

    if owned != LANES or n_row != n_col or n_row & (n_row - 1) or n_row < 4:
        fill = -owned % LANES
        picked = jnp.pad(picked, ((0, 0), (0, fill), (0, 0)))
        keep = jnp.pad(keep, ((0, 0), (0, fill)))
        z = whiten(picked, keep)[:, :, :owned]
        first = lax.all_gather(z, "col", axis=2, tiled=True)
        second = lax.psum(jnp.where(row == col, first, 0).astype(first.dtype), "row")
        nr, nc = tile_r // LANES, tile_c // LANES
        rows = jnp.split(first, nr, axis=2)
        cols = [[(v, [0])] for v in jnp.split(second, nc, axis=2)]
        pairs = [(r, c) for r in range(nr) for c in range(nc)]
        return correlate(rows, cols, pairs, table, jnp.stack([row, col, 0 * col, 0 * col]), shape, None)

    n = n_col
    ring = [(j, (j - 1) % n) for j in range(n)]
    here = jnp.stack([row, col, col, row ^ col])

    def step(pairs, out):
        return correlate(rows, cols, pairs, table, here, shape, out)

    def spread(v, got, held):
        bit = n_row // 2
        while bit > 1:
            v = jnp.where(((row ^ col) & bit) == 0, v, got)
            bit //= 2
            got = hop(v, bit, held, n_col)
        return [(v, list(range(0, n_row, 2))), (got, list(range(1, n_row, 2)))]

    def only(v):
        return jnp.where(row == col, v, 0).astype(v.dtype)

    top = n_row // 2
    rows = [whiten(picked, keep)]
    rows.append(lax.ppermute(rows[0], "col", ring))
    held = [{c} for c in range(n_col)]
    cols = [spread(rows[0], hop(only(rows[0]), top, held, n_col), held)]
    out = None
    pairs = [(0, 0), (1, 0)]
    for s in range(2, n + 1):
        if s < n:
            rows.append(lax.ppermute(rows[s - 1], "col", ring))
        if s == 2:
            held = [{c} for c in range(n_col)]
            coming = [hop(only(rows[1]), top, held, n_col)]
        else:
            coming = send(only(rows[s - 1]), n_row, n_col)
        out = step(pairs, out)
        if s < n:
            rows[s] = gate(rows[s], out)
        coming = [gate(v, out) for v in coming]
        if s == 2:
            cols.append(spread(rows[1], coming[0], held))
        else:
            cols.append([(v, [d]) for d, v in enumerate([rows[s - 1], *coming])])
        pairs = [(r, s - 1) for r in range(min(s, n - 1) + 1)] + [(s, c) for c in range(s - 1) if s < n]
    return step(pairs, out)


def solution(mesh):
    return jax.shard_map(
        functools.partial(local, n_row=mesh.shape["row"], n_col=mesh.shape["col"]),
        mesh=mesh,
        in_specs=(
            P(("seg", "row", "col"), None, None),
            P(("seg", "row", "col")),
            P(("seg", "row", "col"), None),
        ),
        out_specs=P(("seg", "row"), "col", None),
        check_vma=False,
    )
```

time: 225 us -> 177 us (0.79); the launches traced: 225 us -> 173 us
  waiting for transfers between devices: 48.8 us -> 24.1 us
  Pallas kernels: 122 us -> 106 us
  other arithmetic: 13.7 us -> 4.93 us
  starting transfers between devices: 36 us -> 30.4 us
  local copies, waits for them, and re-layouts: 4.3 us -> 7.02 us
    ppermute x11 -> x13, waiting for transfers between devices: 48.8 us -> 24.1 us  [the longest x1 11 us: local(): rows.append(lax.ppermute(rows[0], 'col', ring))]
    pallas_call x4, Pallas kernels: 119 us -> 104 us  [correlate(): pl.pallas_call(functools.partial(pairs_kernel, pairs=pairs, nr=len(used_r...]
    concatenate x3 -> x0, other arithmetic: 5.8 us -> none  [the longest x2 3.06 us: local(): jnp.concatenate(cols[s:s + chunk])]
    ppermute x11 -> x13, starting transfers between devices: 36 us -> 30.4 us  [the longest x6 17.2 us: send(): lax.ppermute(v, ('row', 'col'), [(c * n_col + c, (c ^ d) * n_col + c) for...]
    unnamed x8 -> x26, local copies, waits for them, and re-layouts: 0.02 us -> 5.32 us
    select_n x10 -> x6, other arithmetic: 5.27 us -> 1.75 us  [the longest x2 1.46 us: spread(): v = jnp.where((row ^ col) & bit == 0, v, got)]
    reshape x4 -> x0, local copies, waits for them, and re-layouts: 2.57 us -> none  [rectangle(): blocks = jnp.stack([row_block, col_block, row * turn_r + row_block, col *...]
  transfers between devices with their start and end apart: 11 -> 13, of which waited for: 4 -> 3; matrix products, arithmetic and copies ran while one was open for 5% -> 1% of each run, Pallas kernels for 26% -> 45%
where the time goes in v2:
time: 177 us; the launch traced here: 173 us
  Pallas kernels  106 us (60%)
  starting transfers between devices  30.4 us (17%)
  waiting for transfers between devices  24.1 us (14%)
  local copies, waits for them, and re-layouts  7.02 us (4%)
  other arithmetic  4.93 us (3%)
    pallas_call x4, Pallas kernels, correlate(): pl.pallas_call(functools.partial(pairs_kernel, pairs=pairs, nr=len(used_r...  104 us
    ppermute x6, starting transfers between devices, send(): lax.ppermute(v, ('row', 'col'), [(c * n_col + c, (c ^ d) * n_col + c) for...  17.2 us
    ppermute x4, starting transfers between devices, hop(): return lax.ppermute(v, ('row', 'col'), moves)  11.7 us
    ppermute x1, waiting for transfers between devices, local(): rows.append(lax.ppermute(rows[0], 'col', ring))  11 us
    ppermute x4, waiting for transfers between devices, hop(): return lax.ppermute(v, ('row', 'col'), moves)  10.5 us
    unnamed x26, local copies, waits for them, and re-layouts  5.32 us
  transfers between devices with their start and end apart: 13, of which 3 were waited for; matrix products, arithmetic and copies ran while one was open for 1% of the time, Pallas kernels for 45%

profile of v2, /device:TPU:0, one launch (start us, length us, event | category | flops | bytes accessed | tf_op | source)
XLA Modules:
  0.0 173.5 jit_solution(8193941524616378873)
XLA Ops:
  0.0 0.7 fusion.2
  0.7 0.7 convert_bitcast_fusion.keep_ref
  1.4 1.7 fusion.4
  3.1 1.2 fusion.1.raw_ref
  4.2 0.0 copy-start.1
  4.3 0.9 copy-done.1
  5.2 2.9 %whiten.1.refs_0_ = bf16[128,32,128]{2,1,0:T(8,128)(2,1)S(1)} custom-call(bf16[16,128,256]{2,1,0:T(8,128)(2,1)S(1)} %fusion.1.raw_ref, f32[16,128]{1,0:T(8,128)S(1)} %convert_bitcast_fusion.keep_ref, bf16[2,256,256]{2,1,0:T(8,128)(2,1)S(1)} %copy-done.1), custom_call_target="tpu_custom_call" | custom-call | tf_op jit(solution)/shard_map/whiten/pallas_call | solution.py:77
  8.1 0.1 broadcast_select_fusion.3
  8.2 5.8 %collective-permute-start.2 = (bf16[128,32,128]{2,1,0:T(8,128)(2,1)S(1)}, bf16[128,32,128]{2,1,0:T(8,128)(2,1)}, u32[]{:S(2)}, u32[]{:S(2)}) collective-permute-start(bf16[128,32,128]{2,1,0:T(8,128)(2,1)S(1)} %broadcast_select_fusion.3), channel_id=1, source_target_pairs={{0,8},{5,13},{10,2},{15,7},{16,24},{21,29},{26,18},{31,23}} | collective-permute-start | bytes 3145736 | tf_op jit(solution)/shard_map/ppermute | solution.py:253
  14.0 0.9 collective-permute-start
  14.8 10.5 %collective-permute-done.2 = bf16[128,32,128]{2,1,0:T(8,128)(2,1)} collective-permute-done((bf16[128,32,128]{2,1,0:T(8,128)(2,1)S(1)}, bf16[128,32,128]{2,1,0:T(8,128)(2,1)}, u32[]{:S(2)}, u32[]{:S(2)}) %collective-permute-start.2) | collective-permute-done | bytes 1048608 | tf_op jit(solution)/shard_map/ppermute | solution.py:253
  25.3 0.1 broadcast_select_fusion.5.refs_2_.refs_3_.refs_4_
  25.4 1.4 collective-permute-start.3
  26.8 0.7 pad_add_fusion.here_ref
  27.5 11.0 %collective-permute-done.refs_1_ = bf16[128,32,128]{2,1,0:T(8,128)(2,1)S(1)} collective-permute-done((bf16[128,32,128]{2,1,0:T(8,128)(2,1)S(1)}, bf16[128,32,128]{2,1,0:T(8,128)(2,1)S(1)}, u32[]{:S(2)}, u32[]{:S(2)}) %collective-permute-start) | collective-permute-done | bytes 1048608 | tf_op jit(solution)/shard_map/ppermute | solution.py:314
  38.4 0.1 broadcast_select_fusion.2
  38.5 3.2 %collective-permute-start.5 = (bf16[128,32,128]{2,1,0:T(8,128)(2,1)S(1)}, bf16[128,32,128]{2,1,0:T(8,128)(2,1)S(1)}, u32[]{:S(2)}, u32[]{:S(2)}) collective-permute-start(bf16[128,32,128]{2,1,0:T(8,128)(2,1)S(1)} %broadcast_select_fusion.2), channel_id=1, source_target_pairs={{0,8},{5,13},{10,2},{15,7},{16,24},{21,29},{26,18},{31,23}} | collective-permute-start | bytes 3145736 | tf_op jit(solution)/shard_map/ppermute | solution.py:253
  41.7 0.6 collective-permute-start.1
  42.3 0.0 collective-permute-done.3.refs_3_.refs_4_.refs_5_
  42.3 1.0 copy-done.6
  43.3 15.4 %pairs.4.refs_8_ = bf16[512,512,128]{2,1,0:T(8,128)(2,1)} custom-call(s32[4]{0:T(128)} %constant.40.clone.slots_ref, s32[4]{0:T(128)} %pad_add_fusion.here_ref, bf16[128,32,128]{2,1,0:T(8,128)(2,1)} %copy-done, bf16[128,32,128]{2,1,0:T(8,128)(2,1)} %copy-done.2, bf16[128,32,128]{2,1,0:T(8,128)(2,1)} %copy-done.5, bf16[128,32,128]{2,1,0:T(8,128)(2,1)} %copy-done.6, ...), custom_call_target="tpu_custom_call" | custom-call | flops 19000000512 | bytes 8388608 | tf_op jit(solution)/shard_map/pairs/pallas_call | solution.py:224
  58.7 0.0 collective-permute-done.5
  58.7 1.3 broadcast_select_fusion.4.refs_5_.refs_6_
  60.1 1.4 collective-permute-start.6
  61.4 2.7 %collective-permute-done.1.refs_2_.refs_8_ = bf16[128,32,128]{2,1,0:T(8,128)(2,1)S(1)} collective-permute-done((bf16[128,32,128]{2,1,0:T(8,128)(2,1)S(1)}, bf16[128,32,128]{2,1,0:T(8,128)(2,1)S(1)}, u32[]{:S(2)}, u32[]{:S(2)}) %collective-permute-start.1) | collective-permute-done | bytes 1048608 | tf_op jit(solution)/shard_map/ppermute | solution.py:321
  64.1 0.1 broadcast_select_fusion
  64.2 5.6 %collective-permute-start.10 = (bf16[128,32,128]{2,1,0:T(8,128)(2,1)S(1)}, bf16[128,32,128]{2,1,0:T(8,128)(2,1)S(1)}, u32[]{:S(2)}, u32[]{:S(2)}) collective-permute-start(bf16[128,32,128]{2,1,0:T(8,128)(2,1)S(1)} %broadcast_select_fusion), channel_id=1, source_target_pairs={{0,12},{5,9},{10,6},{15,3},{16,28},{21,25},{26,22},{31,19}} | collective-permute-start | bytes 3145736 | tf_op jit(solution)/shard_map/ppermute | solution.py:258
  69.8 2.3 %collective-permute-start.9 = (bf16[128,32,128]{2,1,0:T(8,128)(2,1)S(1)}, bf16[128,32,128]{2,1,0:T(8,128)(2,1)}, u32[]{:S(2)}, u32[]{:S(2)}) collective-permute-start(bf16[128,32,128]{2,1,0:T(8,128)(2,1)S(1)} %broadcast_select_fusion), channel_id=1, source_target_pairs={{0,8},{5,13},{10,2},{15,7},{16,24},{21,29},{26,18},{31,23}} | collective-permute-start | bytes 3145736 | tf_op jit(solution)/shard_map/ppermute | solution.py:258
  72.1 2.4 %collective-permute-start.8 = (bf16[128,32,128]{2,1,0:T(8,128)(2,1)S(1)}, bf16[128,32,128]{2,1,0:T(8,128)(2,1)}, u32[]{:S(2)}, u32[]{:S(2)}) collective-permute-start(bf16[128,32,128]{2,1,0:T(8,128)(2,1)S(1)} %broadcast_select_fusion), channel_id=1, source_target_pairs={{0,4},{5,1},{10,14},{15,11},{16,20},{21,17},{26,30},{31,27}} | collective-permute-start | bytes 3145736 | tf_op jit(solution)/shard_map/ppermute | solution.py:258
  74.5 0.0 collective-permute-start.4
  74.5 0.0 collective-permute-done.6.refs_6_.refs_7_
  74.5 1.1 copy-done.8
  75.6 26.1 %pairs.5.refs_13_ = bf16[512,512,128]{2,1,0:T(8,128)(2,1)} custom-call(s32[8]{0:T(128)} %constant.41.clone.slots_ref, s32[4]{0:T(128)} %pad_add_fusion.here_ref, bf16[128,32,128]{2,1,0:T(8,128)(2,1)} %copy-done, bf16[128,32,128]{2,1,0:T(8,128)(2,1)} %copy-done.2, bf16[128,32,128]{2,1,0:T(8,128)(2,1)} %copy-done.3, ...), custom_call_target="tpu_custom_call", output_to_operand_aliasing={{}: (10, {})} | custom-call | flops 32999999488 | bytes 16777216 | tf_op jit(solution)/shard_map/pairs/pallas_call | solution.py:224
  101.7 0.0 collective-permute-done.4.refs_3_.refs_4_
  101.7 0.1 broadcast_select_fusion.1
  101.8 4.2 %collective-permute-start.12 = (bf16[128,32,128]{2,1,0:T(8,128)(2,1)S(1)}, bf16[128,32,128]{2,1,0:T(8,128)(2,1)S(1)}, u32[]{:S(2)}, u32[]{:S(2)}) collective-permute-start(bf16[128,32,128]{2,1,0:T(8,128)(2,1)S(1)} %broadcast_select_fusion.1), channel_id=1, source_target_pairs={{0,12},{5,9},{10,6},{15,3},{16,28},{21,25},{26,22},{31,19}} | collective-permute-start | bytes 3145736 | tf_op jit(solution)/shard_map/ppermute | solution.py:258
  106.0 1.4 collective-permute-start.11
  107.4 0.0 collective-permute-done.10.refs_11_
  107.4 1.4 collective-permute-start.7
  108.8 0.0 collective-permute-done.9.refs_10_
  108.8 0.0 collective-permute-done.8.refs_9_
  108.8 36.3 %pairs.6.refs_9_ = bf16[512,512,128]{2,1,0:T(8,128)(2,1)} custom-call(s32[12]{0:T(128)} %constant.42.clone.slots_ref, s32[4]{0:T(128)} %pad_add_fusion.here_ref, bf16[128,32,128]{2,1,0:T(8,128)(2,1)} %copy-done, bf16[128,32,128]{2,1,0:T(8,128)(2,1)} %copy-done.2, bf16[128,32,128]{2,1,0:T(8,128)(2,1)} %copy-done.3, ...), custom_call_target="tpu_custom_call", output_to_operand_aliasing={{}: (15, {})} | custom-call | flops 46999998464 | bytes 25165824 | tf_op jit(solution)/shard_map/pairs/pallas_call | solution.py:224
  145.1 0.0 collective-permute-done.12.refs_7_
  145.1 0.0 collective-permute-done.7.refs_5_
  145.1 0.9 copy-done.9
  146.0 0.4 copy-done.10
  146.4 1.0 copy-done.11
  147.4 25.8 %pairs.7 = bf16[512,512,128]{2,1,0:T(8,128)(2,1)} custom-call(s32[8]{0:T(128)} %constant.43.clone.slots_ref, s32[4]{0:T(128)} %pad_add_fusion.here_ref, bf16[128,32,128]{2,1,0:T(8,128)(2,1)} %copy-done, bf16[128,32,128]{2,1,0:T(8,128)(2,1)} %copy-done.2, bf16[128,32,128]{2,1,0:T(8,128)(2,1)} %copy-done.3, ...), custom_call_target="tpu_custom_call", output_to_operand_aliasing={{}: (11, {})} | custom-call | flops 32999999488 | bytes 16777216 | tf_op jit(solution)/shard_map/pairs/pallas_call | solution.py:224
  (20 shorter events, 0.0 us)
Async XLA Ops:
  4.2 1.0 copy-start.1
  8.1 34.2 %copy-start = (bf16[128,32,128]{2,1,0:T(8,128)(2,1)}, bf16[128,32,128]{2,1,0:T(8,128)(2,1)S(1)}, u32[]{:S(2)}) copy-start(bf16[128,32,128]{2,1,0:T(8,128)(2,1)S(1)} %whiten.1.refs_0_) | copy-start | bytes 3145732
  8.2 17.2 %collective-permute-start.2 = (bf16[128,32,128]{2,1,0:T(8,128)(2,1)S(1)}, bf16[128,32,128]{2,1,0:T(8,128)(2,1)}, u32[]{:S(2)}, u32[]{:S(2)}) collective-permute-start(bf16[128,32,128]{2,1,0:T(8,128)(2,1)S(1)} %broadcast_select_fusion.3), channel_id=1, source_target_pairs={{0,8},{5,13},{10,2},{15,7},{16,24},{21,29},{26,18},{31,23}} | collective-permute-start | bytes 3145736 | tf_op jit(solution)/shard_map/ppermute | solution.py:253
  14.0 24.4 %collective-permute-start = (bf16[128,32,128]{2,1,0:T(8,128)(2,1)S(1)}, bf16[128,32,128]{2,1,0:T(8,128)(2,1)S(1)}, u32[]{:S(2)}, u32[]{:S(2)}) collective-permute-start(bf16[128,32,128]{2,1,0:T(8,128)(2,1)S(1)} %whiten.1.refs_0_), channel_id=1, source_target_pairs={{0,3},{1,0},{2,1},{3,2},{4,7},{5,4},{6,5},{7,6},{8,11},{9,8},{10,9... | collective-permute-start | bytes 3145736 | tf_op jit(solution)/shard_map/ppermute | solution.py:314
  25.4 16.9 %copy-start.5 = (bf16[128,32,128]{2,1,0:T(8,128)(2,1)}, bf16[128,32,128]{2,1,0:T(8,128)(2,1)S(1)}, u32[]{:S(2)}) copy-start(bf16[128,32,128]{2,1,0:T(8,128)(2,1)S(1)} %broadcast_select_fusion.5.refs_2_.refs_3_.refs_4_) | copy-start | bytes 3145732
  25.4 16.9 %collective-permute-start.3 = (bf16[128,32,128]{2,1,0:T(8,128)(2,1)S(1)}, bf16[128,32,128]{2,1,0:T(8,128)(2,1)S(1)}, u32[]{:S(2)}, u32[]{:S(2)}) collective-permute-start(bf16[128,32,128]{2,1,0:T(8,128)(2,1)S(1)} %broadcast_select_fusion.5.refs_2_.refs_3_.refs_4_), channel_id=1, source_target_pairs={{0,4},{8,12},{5,1},{13,9},{2,6},{10,14},{7,3},{15,11},{16,20},{24,... | collective-permute-start | bytes 3145736 | tf_op jit(solution)/shard_map/ppermute | solution.py:253
  38.4 3.9 %copy-start.2 = (bf16[128,32,128]{2,1,0:T(8,128)(2,1)}, bf16[128,32,128]{2,1,0:T(8,128)(2,1)S(1)}, u32[]{:S(2)}) copy-start(bf16[128,32,128]{2,1,0:T(8,128)(2,1)S(1)} %collective-permute-done.refs_1_) | copy-start | bytes 3145732
  38.5 20.2 %collective-permute-start.5 = (bf16[128,32,128]{2,1,0:T(8,128)(2,1)S(1)}, bf16[128,32,128]{2,1,0:T(8,128)(2,1)S(1)}, u32[]{:S(2)}, u32[]{:S(2)}) collective-permute-start(bf16[128,32,128]{2,1,0:T(8,128)(2,1)S(1)} %broadcast_select_fusion.2), channel_id=1, source_target_pairs={{0,8},{5,13},{10,2},{15,7},{16,24},{21,29},{26,18},{31,23}} | collective-permute-start | bytes 3145736 | tf_op jit(solution)/shard_map/ppermute | solution.py:253
  41.7 22.4 %collective-permute-start.1 = (bf16[128,32,128]{2,1,0:T(8,128)(2,1)S(1)}, bf16[128,32,128]{2,1,0:T(8,128)(2,1)S(1)}, u32[]{:S(2)}, u32[]{:S(2)}) collective-permute-start(bf16[128,32,128]{2,1,0:T(8,128)(2,1)S(1)} %collective-permute-done.refs_1_), channel_id=1, source_target_pairs={{0,3},{1,0},{2,1},{3,2},{4,7},{5,4},{6,5},{7,6},{8,11},{9,8},{10,9... | collective-permute-start | bytes 3145736 | tf_op jit(solution)/shard_map/ppermute | solution.py:321
  42.3 1.0 copy-start.6
  60.1 14.4 %copy-start.7 = (bf16[128,32,128]{2,1,0:T(8,128)(2,1)}, bf16[128,32,128]{2,1,0:T(8,128)(2,1)S(1)}, u32[]{:S(2)}) copy-start(bf16[128,32,128]{2,1,0:T(8,128)(2,1)S(1)} %broadcast_select_fusion.4.refs_5_.refs_6_) | copy-start | bytes 3145732
  60.1 14.4 %collective-permute-start.6 = (bf16[128,32,128]{2,1,0:T(8,128)(2,1)S(1)}, bf16[128,32,128]{2,1,0:T(8,128)(2,1)S(1)}, u32[]{:S(2)}, u32[]{:S(2)}) collective-permute-start(bf16[128,32,128]{2,1,0:T(8,128)(2,1)S(1)} %broadcast_select_fusion.4.refs_5_.refs_6_), channel_id=1, source_target_pairs={{0,4},{8,12},{5,1},{13,9},{2,6},{10,14},{7,3},{15,11},{16,20},{24,... | collective-permute-start | bytes 3145736 | tf_op jit(solution)/shard_map/ppermute | solution.py:253
  64.1 10.4 %copy-start.3 = (bf16[128,32,128]{2,1,0:T(8,128)(2,1)}, bf16[128,32,128]{2,1,0:T(8,128)(2,1)S(1)}, u32[]{:S(2)}) copy-start(bf16[128,32,128]{2,1,0:T(8,128)(2,1)S(1)} %collective-permute-done.1.refs_2_.refs_8_) | copy-start | bytes 3145732
  64.2 43.2 %collective-permute-start.10 = (bf16[128,32,128]{2,1,0:T(8,128)(2,1)S(1)}, bf16[128,32,128]{2,1,0:T(8,128)(2,1)S(1)}, u32[]{:S(2)}, u32[]{:S(2)}) collective-permute-start(bf16[128,32,128]{2,1,0:T(8,128)(2,1)S(1)} %broadcast_select_fusion), channel_id=1, source_target_pairs={{0,12},{5,9},{10,6},{15,3},{16,28},{21,25},{26,22},{31,19}} | collective-permute-start | bytes 3145736 | tf_op jit(solution)/shard_map/ppermute | solution.py:258
  69.8 38.9 %collective-permute-start.9 = (bf16[128,32,128]{2,1,0:T(8,128)(2,1)S(1)}, bf16[128,32,128]{2,1,0:T(8,128)(2,1)}, u32[]{:S(2)}, u32[]{:S(2)}) collective-permute-start(bf16[128,32,128]{2,1,0:T(8,128)(2,1)S(1)} %broadcast_select_fusion), channel_id=1, source_target_pairs={{0,8},{5,13},{10,2},{15,7},{16,24},{21,29},{26,18},{31,23}} | collective-permute-start | bytes 3145736 | tf_op jit(solution)/shard_map/ppermute | solution.py:258
  72.1 36.7 %collective-permute-start.8 = (bf16[128,32,128]{2,1,0:T(8,128)(2,1)S(1)}, bf16[128,32,128]{2,1,0:T(8,128)(2,1)}, u32[]{:S(2)}, u32[]{:S(2)}) collective-permute-start(bf16[128,32,128]{2,1,0:T(8,128)(2,1)S(1)} %broadcast_select_fusion), channel_id=1, source_target_pairs={{0,4},{5,1},{10,14},{15,11},{16,20},{21,17},{26,30},{31,27}} | collective-permute-start | bytes 3145736 | tf_op jit(solution)/shard_map/ppermute | solution.py:258
  74.5 27.2 %collective-permute-start.4 = (bf16[128,32,128]{2,1,0:T(8,128)(2,1)S(1)}, bf16[128,32,128]{2,1,0:T(8,128)(2,1)S(1)}, u32[]{:S(2)}, u32[]{:S(2)}) collective-permute-start(bf16[128,32,128]{2,1,0:T(8,128)(2,1)S(1)} %collective-permute-done.1.refs_2_.refs_8_), channel_id=1, source_target_pairs={{0,3},{1,0},{2,1},{3,2},{4,7},{5,4},{6,5},{7,6},{8,11},{9,8},{10,9... | collective-permute-start | bytes 3145736 | tf_op jit(solution)/shard_map/ppermute | solution.py:321
  74.5 1.1 copy-start.8
  101.7 7.1 %copy-start.4 = (bf16[128,32,128]{2,1,0:T(8,128)(2,1)}, bf16[128,32,128]{2,1,0:T(8,128)(2,1)S(1)}, u32[]{:S(2)}) copy-start(bf16[128,32,128]{2,1,0:T(8,128)(2,1)S(1)} %collective-permute-done.4.refs_3_.refs_4_) | copy-start | bytes 3145732
  101.8 43.3 %collective-permute-start.12 = (bf16[128,32,128]{2,1,0:T(8,128)(2,1)S(1)}, bf16[128,32,128]{2,1,0:T(8,128)(2,1)S(1)}, u32[]{:S(2)}, u32[]{:S(2)}) collective-permute-start(bf16[128,32,128]{2,1,0:T(8,128)(2,1)S(1)} %broadcast_select_fusion.1), channel_id=1, source_target_pairs={{0,12},{5,9},{10,6},{15,3},{16,28},{21,25},{26,22},{31,19}} | collective-permute-start | bytes 3145736 | tf_op jit(solution)/shard_map/ppermute | solution.py:258
  106.0 39.1 %collective-permute-start.11 = (bf16[128,32,128]{2,1,0:T(8,128)(2,1)S(1)}, bf16[128,32,128]{2,1,0:T(8,128)(2,1)S(1)}, u32[]{:S(2)}, u32[]{:S(2)}) collective-permute-start(bf16[128,32,128]{2,1,0:T(8,128)(2,1)S(1)} %broadcast_select_fusion.1), channel_id=1, source_target_pairs={{0,8},{5,13},{10,2},{15,7},{16,24},{21,29},{26,18},{31,23}} | collective-permute-start | bytes 3145736 | tf_op jit(solution)/shard_map/ppermute | solution.py:258
  107.4 1.4 copy-start.12
  107.4 37.7 %collective-permute-start.7 = (bf16[128,32,128]{2,1,0:T(8,128)(2,1)S(1)}, bf16[128,32,128]{2,1,0:T(8,128)(2,1)S(1)}, u32[]{:S(2)}, u32[]{:S(2)}) collective-permute-start(bf16[128,32,128]{2,1,0:T(8,128)(2,1)S(1)} %broadcast_select_fusion.1), channel_id=1, source_target_pairs={{0,4},{5,1},{10,14},{15,11},{16,20},{21,17},{26,30},{31,27}} | collective-permute-start | bytes 3145736 | tf_op jit(solution)/shard_map/ppermute | solution.py:258
  145.1 1.0 copy-start.9
  145.1 1.3 copy-start.10
  146.4 1.0 copy-start.11

commit v3 on v2

--- a/solution.py
+++ b/solution.py
@@ -13,6 +13,7 @@
 L = 128
 LANES = 128
 PAD = 8
+TAIL = 4
 
 
 def spectrum_tables(samples):
@@ -36,24 +37,37 @@
     return table.T.astype(ml_dtypes.bfloat16)
 
 
-def whiten_kernel(raw_ref, keep_ref, table_ref, z_ref, rows_ref):
-    windows = raw_ref.shape[0]
+def whiten_kernel(pick_ref, raw_ref, clip_ref, table_ref, z_ref, rows_ref, keep_ref, *picked):
+    windows = raw_ref.shape[2]
+    gap = windows + PAD
+    first = pl.program_id(0) * LANES
     half = table_ref.shape[1] // 2
     parts = 2 * windows
     pitch = parts + PAD
     contract = (((1,), (1,)), ((), ()))
+    keep_ref[...] = clip_ref[...].astype(jnp.float32).T
+
+    def pull(j, carry):
+        record = raw_ref[j, lax.rem(pick_ref[first + j], 2)].astype(jnp.float32)
+        start = pl.multiple_of(j * gap, 8)
+        for q, part in enumerate(picked):
+            part[pl.ds(start, windows), :] = record[:, q * LANES : (q + 1) * LANES]
+        return carry
+
+    lax.fori_loop(0, LANES, pull, 0, unroll=8)
 
     def window(w, carry):
-        raw = raw_ref[w]
+        raw = jnp.concatenate([part[pl.ds(w, LANES, stride=gap), :] for part in picked], axis=1)
+        raw = raw.astype(jnp.bfloat16)
         spec = lax.dot_general(table_ref[0], raw, contract, preferred_element_type=jnp.float32)
         spec += lax.dot_general(table_ref[1], raw, contract, preferred_element_type=jnp.float32)
         real, imag = spec[:half], spec[half:]
         power = real * real + imag * imag
         total = power
-        for gap in (1, 2):
-            edge = jnp.zeros((gap, power.shape[1]), jnp.float32)
-            total += jnp.concatenate([power[gap:], edge], axis=0)
-            total += jnp.concatenate([edge, power[:-gap]], axis=0)
+        for far in (1, 2):
+            edge = jnp.zeros((far, power.shape[1]), jnp.float32)
+            total += jnp.concatenate([power[far:], edge], axis=0)
+            total += jnp.concatenate([edge, power[:-far]], axis=0)
         mean = jnp.sum(power, axis=0, keepdims=True) * (1.0 / half)
         denom = jnp.sqrt(total * 0.2 + 0.1 * mean + 1e-06)
         weight = keep_ref[pl.ds(w, 1), :] / denom
@@ -71,23 +85,30 @@
     lax.fori_loop(0, half, narrow, 0, unroll=8)
 
 
-def whiten(picked, keep):
-    windows, channels, samples = picked.shape
+def whiten(raw, pick, clip):
+    channels, _, windows, samples = raw.shape
     half = samples // 2
     return pl.pallas_call(
         whiten_kernel,
-        grid=(channels // LANES,),
-        in_specs=[
-            pl.BlockSpec((windows, LANES, samples), lambda c: (0, c, 0)),
-            pl.BlockSpec((windows, LANES), lambda c: (0, c)),
-            pl.BlockSpec((2, samples, samples), lambda c: (0, 0, 0)),
-        ],
-        out_specs=pl.BlockSpec((half, 2 * windows, LANES), lambda c: (0, 0, c)),
+        grid_spec=pltpu.PrefetchScalarGridSpec(
+            num_scalar_prefetch=1,
+            grid=(channels // LANES,),
+            in_specs=[
+                pl.BlockSpec((LANES, 2, windows, samples), lambda c, p: (c, 0, 0, 0)),
+                pl.BlockSpec((LANES, windows), lambda c, p: (c, 0)),
+                pl.BlockSpec((2, samples, samples), lambda c, p: (0, 0, 0)),
+            ],
+            out_specs=pl.BlockSpec((half, 2 * windows, LANES), lambda c, p: (0, 0, c)),
+            scratch_shapes=[
+                pltpu.VMEM((half * (2 * windows + PAD), LANES), jnp.float32),
+                pltpu.VMEM((windows, LANES), jnp.float32),
+            ]
+            + [pltpu.VMEM((LANES * (windows + PAD), LANES), jnp.float32)] * (samples // LANES),
+        ),
         out_shape=jax.ShapeDtypeStruct((half, 2 * windows, channels), jnp.bfloat16),
-        scratch_shapes=[pltpu.VMEM((half * (2 * windows + PAD), LANES), jnp.float32)],
         compiler_params=pltpu.CompilerParams(vmem_limit_bytes=32 * 2**20),
         name="whiten",
-    )(picked, keep, jnp.asarray(spectrum_tables(samples)))
+    )(pick, raw, clip, jnp.asarray(spectrum_tables(samples)))
 
 
 def pairs_kernel(slots_ref, here_ref, *refs, pairs, nr, routes, nk, turn):
@@ -97,12 +118,12 @@
         cols.append(list(zip(refs[at : at + len(route)], route, strict=True)))
         at += len(route)
     t_ref = refs[at]
-    o_ref, even_ref, odd_ref, a_ref, b_ref, a_sem, b_sem = refs[-7:]
+    out_ref, even_ref, odd_ref, a_ref, b_ref, o_ref, a_sem, b_sem, o_sem, tail_sem = refs[-10:]
     g = pl.program_id(0)
     last = len(pairs)
     half = a_ref.shape[1]
     windows = a_ref.shape[2] // 2
-    chans = o_ref.shape[0]
+    chans = o_ref.shape[1]
     pitch = 2 * half + PAD
     rounds = half // nk
     ni = chans // rounds
@@ -148,49 +169,81 @@
         start = pl.multiple_of(i * pitch, 8)
         return x_ref[pl.ds(start, 2 * half), :].astype(jnp.bfloat16)
 
-    def lag(x_ref, it):
-        for u in range(0, ni, 2):
-            i = it * ni + u
+    def lag(x_ref, o, first, count):
+        for u in range(0, count, 2):
+            i = first + u
             x = jnp.concatenate([slab(x_ref, i), slab(x_ref, i + 1)], axis=1)
             y = jnp.dot(t_ref[...], x, preferred_element_type=jnp.float32).astype(jnp.bfloat16)
-            o_ref[i] = y[:, :LANES].T
-            o_ref[i + 1] = y[:, LANES:].T
-
-    def loop(body):
-        lax.fori_loop(0, rounds, lambda it, carry: (body(it), carry)[1], 0)
-
-    def both_of(new_ref, old_ref, slot):
-        def body(it):
-            lag(old_ref, it)
-            cross(new_ref, it, slot)
-
-        loop(body)
-
-    pl.when(g == 0)(lambda: loop(lambda it: cross(even_ref, it, 0)))
-    if last > 1:
-        middle = (g > 0) & (g < last)
-        pl.when(middle & (g % 2 == 1))(lambda: both_of(odd_ref, even_ref, 1))
-    if last > 2:
-        pl.when(middle & (g % 2 == 0))(lambda: both_of(even_ref, odd_ref, 0))
-    tail_ref = odd_ref if last % 2 == 0 else even_ref
-    pl.when(g == last)(lambda: loop(lambda it: lag(tail_ref, it)))
+            o[i] = y[:, :LANES].T
+            o[i + 1] = y[:, LANES:].T
+
+    def loop(count, body):
+        lax.fori_loop(0, count, lambda it, carry: (body(it), carry)[1], 0)
 
     back = jnp.maximum(g - 1, 0)
-
     block_r, block_c = block_at(back, slots_ref, here_ref, turn)
-    first_r, first_c = here_ref[0] * turn[0], here_ref[1] * turn[1]
-
-    @pl.when((g > 0) & (first_r + block_r == first_c + block_c))
-    def _():
-        def clear(i, carry):
+    same = here_ref[0] * turn[0] + block_r == here_ref[1] * turn[1] + block_c
+    at_r, at_c = pl.multiple_of(block_r * LANES, LANES), pl.multiple_of(block_c * LANES, LANES)
+
+    def write(slot, first, count, sem):
+        return pltpu.make_async_copy(
+            o_ref.at[slot, pl.ds(first, count)],
+            out_ref.at[pl.ds(at_r + first, count), pl.ds(at_c, LANES), :],
+            sem,
+        )
+
+    def clear(o, first, count):
+        def one(u, carry):
+            i = first + u
             start = pl.multiple_of(i // 16 * 16, 16)
-            rows = o_ref[i, pl.ds(start, 16), :]
+            rows = o[i, pl.ds(start, 16), :]
             ids = lax.broadcasted_iota(jnp.int32, rows.shape, 0) + start
             kept = jnp.where(ids == i, 0.0, rows.astype(jnp.float32))
-            o_ref[i, pl.ds(start, 16), :] = kept.astype(jnp.bfloat16)
+            o[i, pl.ds(start, 16), :] = kept.astype(jnp.bfloat16)
             return carry
 
-        lax.fori_loop(0, chans, clear, 0, unroll=8)
+        @pl.when(same)
+        def _():
+            lax.fori_loop(0, count, one, 0, unroll=8)
+
+    def middle(new_ref, old_ref, slot):
+        done = 1 - slot
+        o = o_ref.at[done]
+        pl.when(g >= 3)(lambda: write(done, 0, chans, o_sem.at[done]).wait())
+
+        def body(it):
+            cross(new_ref, it, slot)
+            lag(old_ref, o, it * ni, ni)
+
+        loop(rounds, body)
+        clear(o, 0, chans)
+        write(done, 0, chans, o_sem.at[done]).start()
+
+    pl.when(g == 0)(lambda: loop(rounds, lambda it: cross(even_ref, it, 0)))
+    if last > 1:
+        pl.when((g > 0) & (g < last) & (g % 2 == 1))(lambda: middle(odd_ref, even_ref, 1))
+    if last > 2:
+        pl.when((g > 0) & (g < last) & (g % 2 == 0))(lambda: middle(even_ref, odd_ref, 0))
+
+    @pl.when(g == last)
+    def _():
+        slot = (last - 1) % 2
+        o = o_ref.at[slot]
+        if last >= 3:
+            write(slot, 0, chans, o_sem.at[slot]).wait()
+        part = chans // TAIL
+
+        def body(q):
+            first = pl.multiple_of(q * part, part)
+            lag(odd_ref if slot else even_ref, o, first, part)
+            clear(o, first, part)
+            write(slot, first, part, tail_sem.at[q]).start()
+
+        loop(TAIL, body)
+        if last >= 2:
+            write(1 - slot, 0, chans, o_sem.at[1 - slot]).wait()
+        for q in range(TAIL):
+            write(slot, q * part, part, tail_sem.at[q]).wait()
 
 
 def block_at(step, slots_ref, here_ref, turn):
@@ -203,9 +256,6 @@
     half, parts = rows[0].shape[:2]
     turn = (shape[0] // LANES, shape[1] // LANES)
     slots = jnp.asarray(np.array(pairs, np.int32).reshape(-1))
-
-    def before(g):
-        return jnp.maximum(g - 1, 0)
 
     used_r, used_c = sorted({r for r, _ in pairs}), sorted({c for _, c in pairs})
     pairs = [(used_r.index(r), used_c.index(c)) for r, c in pairs]
@@ -223,18 +273,17 @@
     buffer = pltpu.VMEM((2, half, parts, LANES), jnp.bfloat16)
     return pl.pallas_call(
         functools.partial(
-            pairs_kernel, pairs=pairs, nr=len(used_r), routes=routes, nk=half, turn=turn
+            pairs_kernel, pairs=pairs, nr=len(used_r), routes=routes, nk=half // 2, turn=turn
         ),
         grid_spec=pltpu.PrefetchScalarGridSpec(
             num_scalar_prefetch=2,
             grid=(steps + 1,),
             in_specs=in_specs,
-            out_specs=pl.BlockSpec(
-                (LANES, LANES, shape[2]),
-                lambda g, p, q: (*block_at(before(g), p, q, turn), 0),
-            ),
+            out_specs=whole,
             scratch_shapes=[pltpu.VMEM((LANES * (2 * half + PAD), LANES), jnp.float32)] * 2
-            + [buffer, buffer, pltpu.SemaphoreType.DMA((2,)), pltpu.SemaphoreType.DMA((2,))],
+            + [buffer, buffer, pltpu.VMEM((2, LANES, LANES, shape[2]), jnp.bfloat16)]
+            + [pltpu.SemaphoreType.DMA((2,))] * 3
+            + [pltpu.SemaphoreType.DMA((TAIL,))],
         ),
         out_shape=jax.ShapeDtypeStruct(shape, jnp.bfloat16),
         input_output_aliases=aliases,
@@ -270,19 +319,16 @@
     samples = raw_traces.shape[2]
     half = samples // 2
     row, col = lax.axis_index("row"), lax.axis_index("col")
-    paired = raw_traces.reshape(owned, 2, windows, samples)
-    parity = (channel_pick % 2)[:, None, None]
-    picked = jnp.where(parity == 1, paired[:, 1], paired[:, 0]).transpose(1, 0, 2)
-    keep = clip_mask.astype(jnp.float32).T
+    raw = raw_traces.reshape(owned, 2, windows, samples)
     table = jnp.asarray(lag_table(samples, L, windows))
     tile_r, tile_c = owned * n_col, owned * n_row
     shape = (tile_r, tile_c, L)
 
     if owned != LANES or n_row != n_col or n_row & (n_row - 1) or n_row < 4:
         fill = -owned % LANES
-        picked = jnp.pad(picked, ((0, 0), (0, fill), (0, 0)))
-        keep = jnp.pad(keep, ((0, 0), (0, fill)))
-        z = whiten(picked, keep)[:, :, :owned]
+        raw = jnp.pad(raw, ((0, fill), (0, 0), (0, 0), (0, 0)))
+        pick, clip = jnp.pad(channel_pick, (0, fill)), jnp.pad(clip_mask, ((0, fill), (0, 0)))
+        z = whiten(raw, pick, clip)[:, :, :owned]
         first = lax.all_gather(z, "col", axis=2, tiled=True)
         second = lax.psum(jnp.where(row == col, first, 0).astype(first.dtype), "row")
         nr, nc = tile_r // LANES, tile_c // LANES
@@ -306,14 +352,11 @@
             got = hop(v, bit, held, n_col)
         return [(v, list(range(0, n_row, 2))), (got, list(range(1, n_row, 2)))]
 
-    def only(v):
-        return jnp.where(row == col, v, 0).astype(v.dtype)
-
     top = n_row // 2
-    rows = [whiten(picked, keep)]
+    rows = [whiten(raw, channel_pick, clip_mask)]
     rows.append(lax.ppermute(rows[0], "col", ring))
     held = [{c} for c in range(n_col)]
-    cols = [spread(rows[0], hop(only(rows[0]), top, held, n_col), held)]
+    cols = [spread(rows[0], hop(rows[0], top, held, n_col), held)]
     out = None
     pairs = [(0, 0), (1, 0)]
     for s in range(2, n + 1):
@@ -321,9 +364,9 @@
             rows.append(lax.ppermute(rows[s - 1], "col", ring))
         if s == 2:
             held = [{c} for c in range(n_col)]
-            coming = [hop(only(rows[1]), top, held, n_col)]
+            coming = [hop(rows[1], top, held, n_col)]
         else:
-            coming = send(only(rows[s - 1]), n_row, n_col)
+            coming = send(rows[s - 1], n_row, n_col)
         out = step(pairs, out)
         if s < n:
             rows[s] = gate(rows[s], out)

time: 177 us -> 170 us (0.960); the launches traced: 173 us -> 169 us
  Pallas kernels: 106 us -> 103 us
  other arithmetic: 4.93 us -> 2.07 us
  local copies, waits for them, and re-layouts: 7.02 us -> 9.34 us
  starting transfers between devices: 30.4 us -> 28.3 us
    pallas_call x4, Pallas kernels: 104 us -> 99.5 us  [correlate(): pl.pallas_call(functools.partial(pairs_kernel, pairs=pairs, nr=len(used_r...]
    unnamed x26 -> x33, local copies, waits for them, and re-layouts: 5.32 us -> 9.34 us
    ppermute x6, starting transfers between devices: 17.2 us -> 14.8 us  [send(): lax.ppermute(v, ('row', 'col'), [(c * n_col + c, (c ^ d) * n_col + c) for...]
    transpose x2 -> x0, other arithmetic: 1.86 us -> none  [the longest x1 1.16 us: local(): jnp.where(parity == 1, paired[:, 1], paired[:, 0]).transpose(1, 0, 2)]
  transfers between devices with their start and end apart: 13 -> 13, of which waited for: 3 -> 3; matrix products, arithmetic and copies ran while one was open for 1% -> 1% of each run, Pallas kernels for 45% -> 44%
where the time goes in v3:
time: 170 us; the launch traced here: 169 us
  Pallas kernels  103 us (61%)
  starting transfers between devices  28.3 us (17%)
  waiting for transfers between devices  25.3 us (15%)
  local copies, waits for them, and re-layouts  9.34 us (5%)
  other arithmetic  2.07 us (1%)
    pallas_call x4, Pallas kernels, correlate(): pl.pallas_call(functools.partial(pairs_kernel, pairs=pairs, nr=len(used_r...  99.5 us
    ppermute x6, starting transfers between devices, send(): lax.ppermute(v, ('row', 'col'), [(c * n_col + c, (c ^ d) * n_col + c) for...  14.8 us
    ppermute x4, waiting for transfers between devices, hop(): return lax.ppermute(v, ('row', 'col'), moves)  11.3 us
    ppermute x4, starting transfers between devices, hop(): return lax.ppermute(v, ('row', 'col'), moves)  10.8 us
    ppermute x1, waiting for transfers between devices, local(): rows.append(lax.ppermute(rows[0], 'col', ring))  10.2 us
    unnamed x33, local copies, waits for them, and re-layouts  9.34 us
    pallas_call x1, Pallas kernels, whiten(): pl.pallas_call(whiten_kernel, grid_spec=pltpu.PrefetchScalarGridSpec(num_...  3.98 us
    ppermute x2, waiting for transfers between devices, local(): rows.append(lax.ppermute(rows[s - 1], 'col', ring))  3.79 us
  transfers between devices with their start and end apart: 13, of which 3 were waited for; matrix products, arithmetic and copies ran while one was open for 1% of the time, Pallas kernels for 44%

profile of v3, /device:TPU:0, one launch (start us, length us, event | category | flops | bytes accessed | tf_op | source)
XLA Modules:
  0.0 168.9 jit_solution(6235946526508520134)
XLA Ops:
  0.0 0.8 copy.13.clip_ref
  0.8 1.6 copy-done.1
  2.4 0.9 copy-done.2
  3.3 0.7 copy-done.3
  4.0 4.0 %whiten.1.refs_0_ = bf16[128,32,128]{2,1,0:T(8,128)(2,1)S(1)} custom-call(s32[128]{0:T(128)S(1)} %copy-done.3, bf16[128,2,16,256]{3,2,1,0:T(8,128)(2,1)S(1)} %bitcast.4, s32[128,16]{1,0:T(8,128)S(1)} %copy.13.clip_ref, bf16[2,256,256]{2,1,0:T(8,128)(2,1)S(1)} %copy-done.2), custom_call_target="tpu_custom_call" | custom-call | tf_op jit(solution)/shard_map/whiten/pallas_call | solution.py:91
  8.0 4.9 %collective-permute-start.2 = (bf16[128,32,128]{2,1,0:T(8,128)(2,1)S(1)}, bf16[128,32,128]{2,1,0:T(8,128)(2,1)S(1)}, u32[]{:S(2)}, u32[]{:S(2)}) collective-permute-start(bf16[128,32,128]{2,1,0:T(8,128)(2,1)S(1)} %whiten.1.refs_0_), channel_id=1, source_target_pairs={{0,8},{5,13},{10,2},{15,7},{16,24},{21,29},{26,18},{31,23}} | collective-permute-start | bytes 3145736 | tf_op jit(solution)/shard_map/ppermute | solution.py:302
  12.9 0.9 collective-permute-start
  13.9 11.3 %collective-permute-done.2 = bf16[128,32,128]{2,1,0:T(8,128)(2,1)S(1)} collective-permute-done((bf16[128,32,128]{2,1,0:T(8,128)(2,1)S(1)}, bf16[128,32,128]{2,1,0:T(8,128)(2,1)S(1)}, u32[]{:S(2)}, u32[]{:S(2)}) %collective-permute-start.2) | collective-permute-done | bytes 1048608 | tf_op jit(solution)/shard_map/ppermute | solution.py:302
  25.2 0.1 broadcast_select_fusion.1.refs_2_.refs_3_.refs_4_
  25.3 1.4 collective-permute-start.3
  26.6 0.6 pad_add_fusion.here_ref
  27.3 10.2 %collective-permute-done.refs_1_ = bf16[128,32,128]{2,1,0:T(8,128)(2,1)S(1)} collective-permute-done((bf16[128,32,128]{2,1,0:T(8,128)(2,1)S(1)}, bf16[128,32,128]{2,1,0:T(8,128)(2,1)S(1)}, u32[]{:S(2)}, u32[]{:S(2)}) %collective-permute-start) | collective-permute-done | bytes 1048608 | tf_op jit(solution)/shard_map/ppermute | solution.py:357
  37.4 3.1 %collective-permute-start.5 = (bf16[128,32,128]{2,1,0:T(8,128)(2,1)S(1)}, bf16[128,32,128]{2,1,0:T(8,128)(2,1)S(1)}, u32[]{:S(2)}, u32[]{:S(2)}) collective-permute-start(bf16[128,32,128]{2,1,0:T(8,128)(2,1)S(1)} %collective-permute-done.refs_1_), channel_id=1, source_target_pairs={{0,8},{5,13},{10,2},{15,7},{16,24},{21,29},{26,18},{31,23}} | collective-permute-start | bytes 3145736 | tf_op jit(solution)/shard_map/ppermute | solution.py:302
  40.6 1.3 collective-permute-start.1
  41.9 0.0 collective-permute-done.3.refs_3_.refs_4_.refs_5_
  41.9 0.0 copy-done.5
  41.9 0.0 copy-done.4
  41.9 0.0 copy-start.7
  41.9 1.0 copy-done.7
  42.9 15.2 %pairs.4.refs_8_ = bf16[512,512,128]{2,1,0:T(8,128)(2,1)} custom-call(s32[4]{0:T(128)} %constant.25.clone.slots_ref, s32[4]{0:T(128)} %pad_add_fusion.here_ref, bf16[128,32,128]{2,1,0:T(8,128)(2,1)} %copy-done, bf16[128,32,128]{2,1,0:T(8,128)(2,1)} %copy-done.4, bf16[128,32,128]{2,1,0:T(8,128)(2,1)} %copy-done.5, bf16[128,32,128]{2,1,0:T(8,128)(2,1)} %copy-done.7, ...), custom_call_target="tpu_custom_call" | custom-call | flops 19000000512 | bytes 8388608 | tf_op jit(solution)/shard_map/pairs/pallas_call | solution.py:274
  58.1 0.0 collective-permute-done.5
  58.1 1.3 broadcast_select_fusion.refs_5_.refs_6_
  59.4 1.4 collective-permute-start.6
  60.8 3.8 %collective-permute-done.1.refs_2_.refs_8_ = bf16[128,32,128]{2,1,0:T(8,128)(2,1)S(1)} collective-permute-done((bf16[128,32,128]{2,1,0:T(8,128)(2,1)S(1)}, bf16[128,32,128]{2,1,0:T(8,128)(2,1)S(1)}, u32[]{:S(2)}, u32[]{:S(2)}) %collective-permute-start.1) | collective-permute-done | bytes 1048608 | tf_op jit(solution)/shard_map/ppermute | solution.py:364
  64.6 3.9 %collective-permute-start.10 = (bf16[128,32,128]{2,1,0:T(8,128)(2,1)S(1)}, bf16[128,32,128]{2,1,0:T(8,128)(2,1)S(1)}, u32[]{:S(2)}, u32[]{:S(2)}) collective-permute-start(bf16[128,32,128]{2,1,0:T(8,128)(2,1)S(1)} %collective-permute-done.1.refs_2_.refs_8_), channel_id=1, source_target_pairs={{0,12},{5,9},{10,6},{15,3},{16,28},{21,25},{26,22},{31,19}} | collective-permute-start | bytes 3145736 | tf_op jit(solution)/shard_map/ppermute | solution.py:307
  68.5 1.4 collective-permute-start.9
  69.9 2.4 %collective-permute-start.8 = (bf16[128,32,128]{2,1,0:T(8,128)(2,1)S(1)}, bf16[128,32,128]{2,1,0:T(8,128)(2,1)}, u32[]{:S(2)}, u32[]{:S(2)}) collective-permute-start(bf16[128,32,128]{2,1,0:T(8,128)(2,1)S(1)} %collective-permute-done.1.refs_2_.refs_8_), channel_id=1, source_target_pairs={{0,4},{5,1},{10,14},{15,11},{16,20},{21,17},{26,30},{31,27}} | collective-permute-start | bytes 3145736 | tf_op jit(solution)/shard_map/ppermute | solution.py:307
  72.2 0.4 collective-permute-start.4
  72.6 0.0 collective-permute-done.6.refs_6_.refs_7_
  72.6 0.0 copy-done.9
  72.6 1.1 copy-done.10
  73.7 24.9 %pairs.5.refs_13_ = bf16[512,512,128]{2,1,0:T(8,128)(2,1)} custom-call(s32[8]{0:T(128)} %constant.26.clone.slots_ref, s32[4]{0:T(128)} %pad_add_fusion.here_ref, bf16[128,32,128]{2,1,0:T(8,128)(2,1)} %copy-done, bf16[128,32,128]{2,1,0:T(8,128)(2,1)} %copy-done.4, bf16[128,32,128]{2,1,0:T(8,128)(2,1)} %copy-done.6, ...), custom_call_target="tpu_custom_call", output_to_operand_aliasing={{}: (10, {})} | custom-call | flops 32999999488 | bytes 16777216 | tf_op jit(solution)/shard_map/pairs/pallas_call | solution.py:274
  98.6 0.0 collective-permute-done.4.refs_3_.refs_4_
  98.6 4.3 %collective-permute-start.12 = (bf16[128,32,128]{2,1,0:T(8,128)(2,1)S(1)}, bf16[128,32,128]{2,1,0:T(8,128)(2,1)S(1)}, u32[]{:S(2)}, u32[]{:S(2)}) collective-permute-start(bf16[128,32,128]{2,1,0:T(8,128)(2,1)S(1)} %collective-permute-done.4.refs_3_.refs_4_), channel_id=1, source_target_pairs={{0,12},{5,9},{10,6},{15,3},{16,28},{21,25},{26,22},{31,19}} | collective-permute-start | bytes 3145736 | tf_op jit(solution)/shard_map/ppermute | solution.py:307
  102.9 1.4 collective-permute-start.11
  104.3 0.0 collective-permute-done.10.refs_11_
  104.3 1.6 collective-permute-start.7
  105.9 0.0 collective-permute-done.9.refs_10_
  105.9 0.0 collective-permute-done.8.refs_9_
  106.0 1.0 copy-done.15
  106.9 34.4 %pairs.6.refs_9_ = bf16[512,512,128]{2,1,0:T(8,128)(2,1)} custom-call(s32[12]{0:T(128)} %constant.27.clone.slots_ref, s32[4]{0:T(128)} %pad_add_fusion.here_ref, bf16[128,32,128]{2,1,0:T(8,128)(2,1)} %copy-done, bf16[128,32,128]{2,1,0:T(8,128)(2,1)} %copy-done.4, bf16[128,32,128]{2,1,0:T(8,128)(2,1)} %copy-done.6, ...), custom_call_target="tpu_custom_call", output_to_operand_aliasing={{}: (15, {})} | custom-call | flops 46999998464 | bytes 25165824 | tf_op jit(solution)/shard_map/pairs/pallas_call | solution.py:274
  141.3 0.0 collective-permute-done.12.refs_7_
  141.3 0.0 collective-permute-done.11.refs_6_
  141.4 0.0 collective-permute-done.7.refs_5_
  141.4 0.9 copy-done.11
  142.3 0.4 copy-done.12
  142.7 1.0 copy-done.13
  143.7 25.0 %pairs.7 = bf16[512,512,128]{2,1,0:T(8,128)(2,1)} custom-call(s32[8]{0:T(128)} %constant.28.clone.slots_ref, s32[4]{0:T(128)} %pad_add_fusion.here_ref, bf16[128,32,128]{2,1,0:T(8,128)(2,1)} %copy-done, bf16[128,32,128]{2,1,0:T(8,128)(2,1)} %copy-done.4, bf16[128,32,128]{2,1,0:T(8,128)(2,1)} %copy-done.6, ...), custom_call_target="tpu_custom_call", output_to_operand_aliasing={{}: (11, {})} | custom-call | flops 32999999488 | bytes 16777216 | tf_op jit(solution)/shard_map/pairs/pallas_call | solution.py:274
  (19 shorter events, 0.0 us)
Async XLA Ops:
  0.8 1.6 copy-start.1
  2.4 0.9 copy-start.2
  3.3 0.7 copy-start.3
  8.0 33.9 %copy-start = (bf16[128,32,128]{2,1,0:T(8,128)(2,1)}, bf16[128,32,128]{2,1,0:T(8,128)(2,1)S(1)}, u32[]{:S(2)}) copy-start(bf16[128,32,128]{2,1,0:T(8,128)(2,1)S(1)} %whiten.1.refs_0_) | copy-start | bytes 3145732
  8.0 17.2 %collective-permute-start.2 = (bf16[128,32,128]{2,1,0:T(8,128)(2,1)S(1)}, bf16[128,32,128]{2,1,0:T(8,128)(2,1)S(1)}, u32[]{:S(2)}, u32[]{:S(2)}) collective-permute-start(bf16[128,32,128]{2,1,0:T(8,128)(2,1)S(1)} %whiten.1.refs_0_), channel_id=1, source_target_pairs={{0,8},{5,13},{10,2},{15,7},{16,24},{21,29},{26,18},{31,23}} | collective-permute-start | bytes 3145736 | tf_op jit(solution)/shard_map/ppermute | solution.py:302
  12.9 24.5 %collective-permute-start = (bf16[128,32,128]{2,1,0:T(8,128)(2,1)S(1)}, bf16[128,32,128]{2,1,0:T(8,128)(2,1)S(1)}, u32[]{:S(2)}, u32[]{:S(2)}) collective-permute-start(bf16[128,32,128]{2,1,0:T(8,128)(2,1)S(1)} %whiten.1.refs_0_), channel_id=1, source_target_pairs={{0,3},{1,0},{2,1},{3,2},{4,7},{5,4},{6,5},{7,6},{8,11},{9,8},{10,9... | collective-permute-start | bytes 3145736 | tf_op jit(solution)/shard_map/ppermute | solution.py:357
  25.3 16.6 %copy-start.5 = (bf16[128,32,128]{2,1,0:T(8,128)(2,1)}, bf16[128,32,128]{2,1,0:T(8,128)(2,1)S(1)}, u32[]{:S(2)}) copy-start(bf16[128,32,128]{2,1,0:T(8,128)(2,1)S(1)} %broadcast_select_fusion.1.refs_2_.refs_3_.refs_4_) | copy-start | bytes 3145732
  25.3 16.6 %collective-permute-start.3 = (bf16[128,32,128]{2,1,0:T(8,128)(2,1)S(1)}, bf16[128,32,128]{2,1,0:T(8,128)(2,1)S(1)}, u32[]{:S(2)}, u32[]{:S(2)}) collective-permute-start(bf16[128,32,128]{2,1,0:T(8,128)(2,1)S(1)} %broadcast_select_fusion.1.refs_2_.refs_3_.refs_4_), channel_id=1, source_target_pairs={{0,4},{8,12},{5,1},{13,9},{2,6},{10,14},{7,3},{15,11},{16,20},{24,... | collective-permute-start | bytes 3145736 | tf_op jit(solution)/shard_map/ppermute | solution.py:302
  37.4 4.5 %copy-start.4 = (bf16[128,32,128]{2,1,0:T(8,128)(2,1)}, bf16[128,32,128]{2,1,0:T(8,128)(2,1)S(1)}, u32[]{:S(2)}) copy-start(bf16[128,32,128]{2,1,0:T(8,128)(2,1)S(1)} %collective-permute-done.refs_1_) | copy-start | bytes 3145732
  37.4 20.6 %collective-permute-start.5 = (bf16[128,32,128]{2,1,0:T(8,128)(2,1)S(1)}, bf16[128,32,128]{2,1,0:T(8,128)(2,1)S(1)}, u32[]{:S(2)}, u32[]{:S(2)}) collective-permute-start(bf16[128,32,128]{2,1,0:T(8,128)(2,1)S(1)} %collective-permute-done.refs_1_), channel_id=1, source_target_pairs={{0,8},{5,13},{10,2},{15,7},{16,24},{21,29},{26,18},{31,23}} | collective-permute-start | bytes 3145736 | tf_op jit(solution)/shard_map/ppermute | solution.py:302
  40.6 24.0 %collective-permute-start.1 = (bf16[128,32,128]{2,1,0:T(8,128)(2,1)S(1)}, bf16[128,32,128]{2,1,0:T(8,128)(2,1)S(1)}, u32[]{:S(2)}, u32[]{:S(2)}) collective-permute-start(bf16[128,32,128]{2,1,0:T(8,128)(2,1)S(1)} %collective-permute-done.refs_1_), channel_id=1, source_target_pairs={{0,3},{1,0},{2,1},{3,2},{4,7},{5,4},{6,5},{7,6},{8,11},{9,8},{10,9... | collective-permute-start | bytes 3145736 | tf_op jit(solution)/shard_map/ppermute | solution.py:364
  41.9 1.0 copy-start.7
  59.4 13.2 %copy-start.9 = (bf16[128,32,128]{2,1,0:T(8,128)(2,1)}, bf16[128,32,128]{2,1,0:T(8,128)(2,1)S(1)}, u32[]{:S(2)}) copy-start(bf16[128,32,128]{2,1,0:T(8,128)(2,1)S(1)} %broadcast_select_fusion.refs_5_.refs_6_) | copy-start | bytes 3145732
  59.4 13.2 %collective-permute-start.6 = (bf16[128,32,128]{2,1,0:T(8,128)(2,1)S(1)}, bf16[128,32,128]{2,1,0:T(8,128)(2,1)S(1)}, u32[]{:S(2)}, u32[]{:S(2)}) collective-permute-start(bf16[128,32,128]{2,1,0:T(8,128)(2,1)S(1)} %broadcast_select_fusion.refs_5_.refs_6_), channel_id=1, source_target_pairs={{0,4},{8,12},{5,1},{13,9},{2,6},{10,14},{7,3},{15,11},{16,20},{24,... | collective-permute-start | bytes 3145736 | tf_op jit(solution)/shard_map/ppermute | solution.py:302
  64.6 8.1 %copy-start.6 = (bf16[128,32,128]{2,1,0:T(8,128)(2,1)}, bf16[128,32,128]{2,1,0:T(8,128)(2,1)S(1)}, u32[]{:S(2)}) copy-start(bf16[128,32,128]{2,1,0:T(8,128)(2,1)S(1)} %collective-permute-done.1.refs_2_.refs_8_) | copy-start | bytes 3145732
  64.6 39.7 %collective-permute-start.10 = (bf16[128,32,128]{2,1,0:T(8,128)(2,1)S(1)}, bf16[128,32,128]{2,1,0:T(8,128)(2,1)S(1)}, u32[]{:S(2)}, u32[]{:S(2)}) collective-permute-start(bf16[128,32,128]{2,1,0:T(8,128)(2,1)S(1)} %collective-permute-done.1.refs_2_.refs_8_), channel_id=1, source_target_pairs={{0,12},{5,9},{10,6},{15,3},{16,28},{21,25},{26,22},{31,19}} | collective-permute-start | bytes 3145736 | tf_op jit(solution)/shard_map/ppermute | solution.py:307
  68.5 37.4 %collective-permute-start.9 = (bf16[128,32,128]{2,1,0:T(8,128)(2,1)S(1)}, bf16[128,32,128]{2,1,0:T(8,128)(2,1)S(1)}, u32[]{:S(2)}, u32[]{:S(2)}) collective-permute-start(bf16[128,32,128]{2,1,0:T(8,128)(2,1)S(1)} %collective-permute-done.1.refs_2_.refs_8_), channel_id=1, source_target_pairs={{0,8},{5,13},{10,2},{15,7},{16,24},{21,29},{26,18},{31,23}} | collective-permute-start | bytes 3145736 | tf_op jit(solution)/shard_map/ppermute | solution.py:307
  69.9 36.1 %collective-permute-start.8 = (bf16[128,32,128]{2,1,0:T(8,128)(2,1)S(1)}, bf16[128,32,128]{2,1,0:T(8,128)(2,1)}, u32[]{:S(2)}, u32[]{:S(2)}) collective-permute-start(bf16[128,32,128]{2,1,0:T(8,128)(2,1)S(1)} %collective-permute-done.1.refs_2_.refs_8_), channel_id=1, source_target_pairs={{0,4},{5,1},{10,14},{15,11},{16,20},{21,17},{26,30},{31,27}} | collective-permute-start | bytes 3145736 | tf_op jit(solution)/shard_map/ppermute | solution.py:307
  72.2 26.4 %collective-permute-start.4 = (bf16[128,32,128]{2,1,0:T(8,128)(2,1)S(1)}, bf16[128,32,128]{2,1,0:T(8,128)(2,1)S(1)}, u32[]{:S(2)}, u32[]{:S(2)}) collective-permute-start(bf16[128,32,128]{2,1,0:T(8,128)(2,1)S(1)} %collective-permute-done.1.refs_2_.refs_8_), channel_id=1, source_target_pairs={{0,3},{1,0},{2,1},{3,2},{4,7},{5,4},{6,5},{7,6},{8,11},{9,8},{10,9... | collective-permute-start | bytes 3145736 | tf_op jit(solution)/shard_map/ppermute | solution.py:364
  72.6 1.1 copy-start.10
  98.6 7.3 %copy-start.8 = (bf16[128,32,128]{2,1,0:T(8,128)(2,1)}, bf16[128,32,128]{2,1,0:T(8,128)(2,1)S(1)}, u32[]{:S(2)}) copy-start(bf16[128,32,128]{2,1,0:T(8,128)(2,1)S(1)} %collective-permute-done.4.refs_3_.refs_4_) | copy-start | bytes 3145732
  98.6 42.7 %collective-permute-start.12 = (bf16[128,32,128]{2,1,0:T(8,128)(2,1)S(1)}, bf16[128,32,128]{2,1,0:T(8,128)(2,1)S(1)}, u32[]{:S(2)}, u32[]{:S(2)}) collective-permute-start(bf16[128,32,128]{2,1,0:T(8,128)(2,1)S(1)} %collective-permute-done.4.refs_3_.refs_4_), channel_id=1, source_target_pairs={{0,12},{5,9},{10,6},{15,3},{16,28},{21,25},{26,22},{31,19}} | collective-permute-start | bytes 3145736 | tf_op jit(solution)/shard_map/ppermute | solution.py:307
  102.9 38.4 %collective-permute-start.11 = (bf16[128,32,128]{2,1,0:T(8,128)(2,1)S(1)}, bf16[128,32,128]{2,1,0:T(8,128)(2,1)S(1)}, u32[]{:S(2)}, u32[]{:S(2)}) collective-permute-start(bf16[128,32,128]{2,1,0:T(8,128)(2,1)S(1)} %collective-permute-done.4.refs_3_.refs_4_), channel_id=1, source_target_pairs={{0,8},{5,13},{10,2},{15,7},{16,24},{21,29},{26,18},{31,23}} | collective-permute-start | bytes 3145736 | tf_op jit(solution)/shard_map/ppermute | solution.py:307
  104.3 1.6 copy-start.14
  104.3 37.0 %collective-permute-start.7 = (bf16[128,32,128]{2,1,0:T(8,128)(2,1)S(1)}, bf16[128,32,128]{2,1,0:T(8,128)(2,1)S(1)}, u32[]{:S(2)}, u32[]{:S(2)}) collective-permute-start(bf16[128,32,128]{2,1,0:T(8,128)(2,1)S(1)} %collective-permute-done.4.refs_3_.refs_4_), channel_id=1, source_target_pairs={{0,4},{5,1},{10,14},{15,11},{16,20},{21,17},{26,30},{31,27}} | collective-permute-start | bytes 3145736 | tf_op jit(solution)/shard_map/ppermute | solution.py:307
  105.9 1.0 copy-start.15
  141.3 1.0 copy-start.11
  141.3 1.3 copy-start.12
  142.7 1.0 copy-start.13

commit v4 on v3

--- a/solution.py
+++ b/solution.py
@@ -37,7 +37,7 @@
     return table.T.astype(ml_dtypes.bfloat16)
 
 
-def whiten_kernel(pick_ref, raw_ref, clip_ref, table_ref, z_ref, rows_ref, keep_ref, *picked):
+def whiten_kernel(pick_ref, raw_ref, clip_ref, table_ref, z_ref, rows_ref, *picked):
     windows = raw_ref.shape[2]
     gap = windows + PAD
     first = pl.program_id(0) * LANES
@@ -45,7 +45,6 @@
     parts = 2 * windows
     pitch = parts + PAD
     contract = (((1,), (1,)), ((), ()))
-    keep_ref[...] = clip_ref[...].astype(jnp.float32).T
 
     def pull(j, carry):
         record = raw_ref[j, lax.rem(pick_ref[first + j], 2)].astype(jnp.float32)
@@ -70,7 +69,7 @@
             total += jnp.concatenate([edge, power[:-far]], axis=0)
         mean = jnp.sum(power, axis=0, keepdims=True) * (1.0 / half)
         denom = jnp.sqrt(total * 0.2 + 0.1 * mean + 1e-06)
-        weight = keep_ref[pl.ds(w, 1), :] / denom
+        weight = clip_ref[pl.ds(w, 1), :].astype(jnp.float32) / denom
         rows_ref[pl.ds(w, half, stride=pitch), :] = real * weight
         rows_ref[pl.ds(windows + w, half, stride=pitch), :] = imag * weight
         return carry
@@ -95,13 +94,12 @@
             grid=(channels // LANES,),
             in_specs=[
                 pl.BlockSpec((LANES, 2, windows, samples), lambda c, p: (c, 0, 0, 0)),
-                pl.BlockSpec((LANES, windows), lambda c, p: (c, 0)),
+                pl.BlockSpec((windows, LANES), lambda c, p: (0, c)),
                 pl.BlockSpec((2, samples, samples), lambda c, p: (0, 0, 0)),
             ],
             out_specs=pl.BlockSpec((half, 2 * windows, LANES), lambda c, p: (0, 0, c)),
             scratch_shapes=[
                 pltpu.VMEM((half * (2 * windows + PAD), LANES), jnp.float32),
-                pltpu.VMEM((windows, LANES), jnp.float32),
             ]
             + [pltpu.VMEM((LANES * (windows + PAD), LANES), jnp.float32)] * (samples // LANES),
         ),
@@ -320,6 +318,7 @@
     half = samples // 2
     row, col = lax.axis_index("row"), lax.axis_index("col")
     raw = raw_traces.reshape(owned, 2, windows, samples)
+    clip = clip_mask.T
     table = jnp.asarray(lag_table(samples, L, windows))
     tile_r, tile_c = owned * n_col, owned * n_row
     shape = (tile_r, tile_c, L)
@@ -327,7 +326,7 @@
     if owned != LANES or n_row != n_col or n_row & (n_row - 1) or n_row < 4:
         fill = -owned % LANES
         raw = jnp.pad(raw, ((0, fill), (0, 0), (0, 0), (0, 0)))
-        pick, clip = jnp.pad(channel_pick, (0, fill)), jnp.pad(clip_mask, ((0, fill), (0, 0)))
+        pick, clip = jnp.pad(channel_pick, (0, fill)), jnp.pad(clip, ((0, 0), (0, fill)))
         z = whiten(raw, pick, clip)[:, :, :owned]
         first = lax.all_gather(z, "col", axis=2, tiled=True)
         second = lax.psum(jnp.where(row == col, first, 0).astype(first.dtype), "row")
@@ -353,7 +352,7 @@
         return [(v, list(range(0, n_row, 2))), (got, list(range(1, n_row, 2)))]
 
     top = n_row // 2
-    rows = [whiten(raw, channel_pick, clip_mask)]
+    rows = [whiten(raw, channel_pick, clip)]
     rows.append(lax.ppermute(rows[0], "col", ring))
     held = [{c} for c in range(n_col)]
     cols = [spread(rows[0], hop(rows[0], top, held, n_col), held)]

time: 170 us -> 169 us (level)
    unnamed x33 -> x34, local copies, waits for them, and re-layouts: 9.34 us -> 9.24 us
where the time goes in v4:
time: 169 us
  Pallas kernels  103 us (61%)
  starting transfers between devices  28.2 us (17%)
  waiting for transfers between devices  25.3 us (15%)
  local copies, waits for them, and re-layouts  9.24 us (5%)
  other arithmetic  2.13 us (1%)
    pallas_call x4, Pallas kernels, correlate(): pl.pallas_call(functools.partial(pairs_kernel, pairs=pairs, nr=len(used_r...  99.4 us
    ppermute x6, starting transfers between devices, send(): lax.ppermute(v, ('row', 'col'), [(c * n_col + c, (c ^ d) * n_col + c) for...  14.9 us
    ppermute x4, waiting for transfers between devices, hop(): return lax.ppermute(v, ('row', 'col'), moves)  11.3 us
    ppermute x4, starting transfers between devices, hop(): return lax.ppermute(v, ('row', 'col'), moves)  10.8 us
    ppermute x1, waiting for transfers between devices, local(): rows.append(lax.ppermute(rows[0], 'col', ring))  10.1 us
    unnamed x34, local copies, waits for them, and re-layouts  9.24 us
    pallas_call x1, Pallas kernels, whiten(): pl.pallas_call(whiten_kernel, grid_spec=pltpu.PrefetchScalarGridSpec(num_...  3.93 us
    ppermute x2, waiting for transfers between devices, local(): rows.append(lax.ppermute(rows[s - 1], 'col', ring))  3.87 us
  transfers between devices with their start and end apart: 13, of which 3 were waited for; matrix products, arithmetic and copies ran while one was open for 1% of the time, Pallas kernels for 44%

profile of v4, /device:TPU:0, one launch (start us, length us, event | category | flops | bytes accessed | tf_op | source)
XLA Modules:
  0.0 168.8 jit_solution(904079583198482833)
XLA Ops:
  0.0 1.6 copy-done.1
  1.6 0.9 copy-done.2
  2.5 0.7 copy-done.3
  3.2 0.7 copy-done.4
  3.9 3.9 %whiten.1.refs_0_ = bf16[128,32,128]{2,1,0:T(8,128)(2,1)S(1)} custom-call(s32[128]{0:T(128)S(1)} %copy-done.4, bf16[128,2,16,256]{3,2,1,0:T(8,128)(2,1)S(1)} %bitcast.5, s32[16,128]{1,0:T(8,128)S(1)} %bitcast.6, bf16[2,256,256]{2,1,0:T(8,128)(2,1)S(1)} %copy-done.2), custom_call_target="tpu_custom_call" | custom-call | tf_op jit(solution)/shard_map/whiten/pallas_call | solution.py:90
  7.8 4.9 %collective-permute-start.2 = (bf16[128,32,128]{2,1,0:T(8,128)(2,1)S(1)}, bf16[128,32,128]{2,1,0:T(8,128)(2,1)S(1)}, u32[]{:S(2)}, u32[]{:S(2)}) collective-permute-start(bf16[128,32,128]{2,1,0:T(8,128)(2,1)S(1)} %whiten.1.refs_0_), channel_id=1, source_target_pairs={{0,8},{5,13},{10,2},{15,7},{16,24},{21,29},{26,18},{31,23}} | collective-permute-start | bytes 3145736 | tf_op jit(solution)/shard_map/ppermute | solution.py:300
  12.8 0.9 collective-permute-start
  13.7 11.3 %collective-permute-done.2 = bf16[128,32,128]{2,1,0:T(8,128)(2,1)S(1)} collective-permute-done((bf16[128,32,128]{2,1,0:T(8,128)(2,1)S(1)}, bf16[128,32,128]{2,1,0:T(8,128)(2,1)S(1)}, u32[]{:S(2)}, u32[]{:S(2)}) %collective-permute-start.2) | collective-permute-done | bytes 1048608 | tf_op jit(solution)/shard_map/ppermute | solution.py:300
  25.0 0.1 broadcast_select_fusion.1.refs_2_.refs_3_.refs_4_
  25.1 0.0 copy-start.6
  25.1 1.4 collective-permute-start.3
  26.5 0.7 pad_add_fusion.here_ref
  27.2 10.1 %collective-permute-done.refs_1_ = bf16[128,32,128]{2,1,0:T(8,128)(2,1)S(1)} collective-permute-done((bf16[128,32,128]{2,1,0:T(8,128)(2,1)S(1)}, bf16[128,32,128]{2,1,0:T(8,128)(2,1)S(1)}, u32[]{:S(2)}, u32[]{:S(2)}) %collective-permute-start) | collective-permute-done | bytes 1048608 | tf_op jit(solution)/shard_map/ppermute | solution.py:356
  37.3 3.1 %collective-permute-start.5 = (bf16[128,32,128]{2,1,0:T(8,128)(2,1)S(1)}, bf16[128,32,128]{2,1,0:T(8,128)(2,1)S(1)}, u32[]{:S(2)}, u32[]{:S(2)}) collective-permute-start(bf16[128,32,128]{2,1,0:T(8,128)(2,1)S(1)} %collective-permute-done.refs_1_), channel_id=1, source_target_pairs={{0,8},{5,13},{10,2},{15,7},{16,24},{21,29},{26,18},{31,23}} | collective-permute-start | bytes 3145736 | tf_op jit(solution)/shard_map/ppermute | solution.py:300
  40.4 1.3 collective-permute-start.1
  41.8 0.0 collective-permute-done.3.refs_3_.refs_4_.refs_5_
  41.8 0.0 copy-done
  41.8 1.0 copy-done.8
  42.8 15.2 %pairs.4.refs_8_ = bf16[512,512,128]{2,1,0:T(8,128)(2,1)} custom-call(s32[4]{0:T(128)} %constant.25.clone.slots_ref, s32[4]{0:T(128)} %pad_add_fusion.here_ref, bf16[128,32,128]{2,1,0:T(8,128)(2,1)} %copy-done, bf16[128,32,128]{2,1,0:T(8,128)(2,1)} %copy-done.5, bf16[128,32,128]{2,1,0:T(8,128)(2,1)} %copy-done.6, bf16[128,32,128]{2,1,0:T(8,128)(2,1)} %copy-done.8, ...), custom_call_target="tpu_custom_call" | custom-call | flops 19000000512 | bytes 8388608 | tf_op jit(solution)/shard_map/pairs/pallas_call | solution.py:272
  57.9 0.0 collective-permute-done.5
  58.0 1.3 broadcast_select_fusion.refs_5_.refs_6_
  59.3 0.0 copy-start.10
  59.3 1.4 collective-permute-start.6
  60.7 3.9 %collective-permute-done.1.refs_2_.refs_8_ = bf16[128,32,128]{2,1,0:T(8,128)(2,1)S(1)} collective-permute-done((bf16[128,32,128]{2,1,0:T(8,128)(2,1)S(1)}, bf16[128,32,128]{2,1,0:T(8,128)(2,1)S(1)}, u32[]{:S(2)}, u32[]{:S(2)}) %collective-permute-start.1) | collective-permute-done | bytes 1048608 | tf_op jit(solution)/shard_map/ppermute | solution.py:363
  64.5 4.0 %collective-permute-start.10 = (bf16[128,32,128]{2,1,0:T(8,128)(2,1)S(1)}, bf16[128,32,128]{2,1,0:T(8,128)(2,1)S(1)}, u32[]{:S(2)}, u32[]{:S(2)}) collective-permute-start(bf16[128,32,128]{2,1,0:T(8,128)(2,1)S(1)} %collective-permute-done.1.refs_2_.refs_8_), channel_id=1, source_target_pairs={{0,12},{5,9},{10,6},{15,3},{16,28},{21,25},{26,22},{31,19}} | collective-permute-start | bytes 3145736 | tf_op jit(solution)/shard_map/ppermute | solution.py:305
  68.6 1.4 collective-permute-start.9
  69.9 2.3 %collective-permute-start.8 = (bf16[128,32,128]{2,1,0:T(8,128)(2,1)S(1)}, bf16[128,32,128]{2,1,0:T(8,128)(2,1)}, u32[]{:S(2)}, u32[]{:S(2)}) collective-permute-start(bf16[128,32,128]{2,1,0:T(8,128)(2,1)S(1)} %collective-permute-done.1.refs_2_.refs_8_), channel_id=1, source_target_pairs={{0,4},{5,1},{10,14},{15,11},{16,20},{21,17},{26,30},{31,27}} | collective-permute-start | bytes 3145736 | tf_op jit(solution)/shard_map/ppermute | solution.py:305
  72.3 0.3 collective-permute-start.4
  72.6 0.0 collective-permute-done.6.refs_6_.refs_7_
  72.6 1.1 copy-done.11
  73.7 24.9 %pairs.5.refs_13_ = bf16[512,512,128]{2,1,0:T(8,128)(2,1)} custom-call(s32[8]{0:T(128)} %constant.26.clone.slots_ref, s32[4]{0:T(128)} %pad_add_fusion.here_ref, bf16[128,32,128]{2,1,0:T(8,128)(2,1)} %copy-done, bf16[128,32,128]{2,1,0:T(8,128)(2,1)} %copy-done.5, bf16[128,32,128]{2,1,0:T(8,128)(2,1)} %copy-done.7, ...), custom_call_target="tpu_custom_call", output_to_operand_aliasing={{}: (10, {})} | custom-call | flops 32999999488 | bytes 16777216 | tf_op jit(solution)/shard_map/pairs/pallas_call | solution.py:272
  98.6 0.0 collective-permute-done.4.refs_3_.refs_4_
  98.6 4.3 %collective-permute-start.12 = (bf16[128,32,128]{2,1,0:T(8,128)(2,1)S(1)}, bf16[128,32,128]{2,1,0:T(8,128)(2,1)S(1)}, u32[]{:S(2)}, u32[]{:S(2)}) collective-permute-start(bf16[128,32,128]{2,1,0:T(8,128)(2,1)S(1)} %collective-permute-done.4.refs_3_.refs_4_), channel_id=1, source_target_pairs={{0,12},{5,9},{10,6},{15,3},{16,28},{21,25},{26,22},{31,19}} | collective-permute-start | bytes 3145736 | tf_op jit(solution)/shard_map/ppermute | solution.py:305
  102.9 1.4 collective-permute-start.11
  104.2 0.0 collective-permute-done.10.refs_11_
  104.3 1.6 collective-permute-start.7
  105.8 0.0 collective-permute-done.9.refs_10_
  105.9 0.0 collective-permute-done.8.refs_9_
  105.9 1.0 copy-done.16
  106.9 34.4 %pairs.6.refs_9_ = bf16[512,512,128]{2,1,0:T(8,128)(2,1)} custom-call(s32[12]{0:T(128)} %constant.27.clone.slots_ref, s32[4]{0:T(128)} %pad_add_fusion.here_ref, bf16[128,32,128]{2,1,0:T(8,128)(2,1)} %copy-done, bf16[128,32,128]{2,1,0:T(8,128)(2,1)} %copy-done.5, bf16[128,32,128]{2,1,0:T(8,128)(2,1)} %copy-done.7, ...), custom_call_target="tpu_custom_call", output_to_operand_aliasing={{}: (15, {})} | custom-call | flops 46999998464 | bytes 25165824 | tf_op jit(solution)/shard_map/pairs/pallas_call | solution.py:272
  141.2 0.0 collective-permute-done.12.refs_7_
  141.2 0.0 collective-permute-done.11.refs_6_
  141.3 0.0 copy-start.13
  141.3 0.0 collective-permute-done.7.refs_5_
  141.3 0.9 copy-done.12
  142.2 0.4 copy-done.13
  142.6 1.0 copy-done.14
  143.6 25.0 %pairs.7 = bf16[512,512,128]{2,1,0:T(8,128)(2,1)} custom-call(s32[8]{0:T(128)} %constant.28.clone.slots_ref, s32[4]{0:T(128)} %pad_add_fusion.here_ref, bf16[128,32,128]{2,1,0:T(8,128)(2,1)} %copy-done, bf16[128,32,128]{2,1,0:T(8,128)(2,1)} %copy-done.5, bf16[128,32,128]{2,1,0:T(8,128)(2,1)} %copy-done.7, ...), custom_call_target="tpu_custom_call", output_to_operand_aliasing={{}: (11, {})} | custom-call | flops 32999999488 | bytes 16777216 | tf_op jit(solution)/shard_map/pairs/pallas_call | solution.py:272
  (20 shorter events, 0.0 us)
Async XLA Ops:
  0.0 1.6 copy-start.1
  1.6 0.9 copy-start.2
  2.5 0.7 copy-start.3
  3.2 0.7 copy-start.4
  7.8 33.9 %copy-start = (bf16[128,32,128]{2,1,0:T(8,128)(2,1)}, bf16[128,32,128]{2,1,0:T(8,128)(2,1)S(1)}, u32[]{:S(2)}) copy-start(bf16[128,32,128]{2,1,0:T(8,128)(2,1)S(1)} %whiten.1.refs_0_) | copy-start | bytes 3145732
  7.8 17.2 %collective-permute-start.2 = (bf16[128,32,128]{2,1,0:T(8,128)(2,1)S(1)}, bf16[128,32,128]{2,1,0:T(8,128)(2,1)S(1)}, u32[]{:S(2)}, u32[]{:S(2)}) collective-permute-start(bf16[128,32,128]{2,1,0:T(8,128)(2,1)S(1)} %whiten.1.refs_0_), channel_id=1, source_target_pairs={{0,8},{5,13},{10,2},{15,7},{16,24},{21,29},{26,18},{31,23}} | collective-permute-start | bytes 3145736 | tf_op jit(solution)/shard_map/ppermute | solution.py:300
  12.8 24.5 %collective-permute-start = (bf16[128,32,128]{2,1,0:T(8,128)(2,1)S(1)}, bf16[128,32,128]{2,1,0:T(8,128)(2,1)S(1)}, u32[]{:S(2)}, u32[]{:S(2)}) collective-permute-start(bf16[128,32,128]{2,1,0:T(8,128)(2,1)S(1)} %whiten.1.refs_0_), channel_id=1, source_target_pairs={{0,3},{1,0},{2,1},{3,2},{4,7},{5,4},{6,5},{7,6},{8,11},{9,8},{10,9... | collective-permute-start | bytes 3145736 | tf_op jit(solution)/shard_map/ppermute | solution.py:356
  25.1 16.6 %copy-start.6 = (bf16[128,32,128]{2,1,0:T(8,128)(2,1)}, bf16[128,32,128]{2,1,0:T(8,128)(2,1)S(1)}, u32[]{:S(2)}) copy-start(bf16[128,32,128]{2,1,0:T(8,128)(2,1)S(1)} %broadcast_select_fusion.1.refs_2_.refs_3_.refs_4_) | copy-start | bytes 3145732
  25.1 16.6 %collective-permute-start.3 = (bf16[128,32,128]{2,1,0:T(8,128)(2,1)S(1)}, bf16[128,32,128]{2,1,0:T(8,128)(2,1)S(1)}, u32[]{:S(2)}, u32[]{:S(2)}) collective-permute-start(bf16[128,32,128]{2,1,0:T(8,128)(2,1)S(1)} %broadcast_select_fusion.1.refs_2_.refs_3_.refs_4_), channel_id=1, source_target_pairs={{0,4},{8,12},{5,1},{13,9},{2,6},{10,14},{7,3},{15,11},{16,20},{24,... | collective-permute-start | bytes 3145736 | tf_op jit(solution)/shard_map/ppermute | solution.py:300
  37.3 4.5 %copy-start.5 = (bf16[128,32,128]{2,1,0:T(8,128)(2,1)}, bf16[128,32,128]{2,1,0:T(8,128)(2,1)S(1)}, u32[]{:S(2)}) copy-start(bf16[128,32,128]{2,1,0:T(8,128)(2,1)S(1)} %collective-permute-done.refs_1_) | copy-start | bytes 3145732
  37.3 20.7 %collective-permute-start.5 = (bf16[128,32,128]{2,1,0:T(8,128)(2,1)S(1)}, bf16[128,32,128]{2,1,0:T(8,128)(2,1)S(1)}, u32[]{:S(2)}, u32[]{:S(2)}) collective-permute-start(bf16[128,32,128]{2,1,0:T(8,128)(2,1)S(1)} %collective-permute-done.refs_1_), channel_id=1, source_target_pairs={{0,8},{5,13},{10,2},{15,7},{16,24},{21,29},{26,18},{31,23}} | collective-permute-start | bytes 3145736 | tf_op jit(solution)/shard_map/ppermute | solution.py:300
  40.4 24.1 %collective-permute-start.1 = (bf16[128,32,128]{2,1,0:T(8,128)(2,1)S(1)}, bf16[128,32,128]{2,1,0:T(8,128)(2,1)S(1)}, u32[]{:S(2)}, u32[]{:S(2)}) collective-permute-start(bf16[128,32,128]{2,1,0:T(8,128)(2,1)S(1)} %collective-permute-done.refs_1_), channel_id=1, source_target_pairs={{0,3},{1,0},{2,1},{3,2},{4,7},{5,4},{6,5},{7,6},{8,11},{9,8},{10,9... | collective-permute-start | bytes 3145736 | tf_op jit(solution)/shard_map/ppermute | solution.py:363
  41.8 1.0 copy-start.8
  59.3 13.3 %copy-start.10 = (bf16[128,32,128]{2,1,0:T(8,128)(2,1)}, bf16[128,32,128]{2,1,0:T(8,128)(2,1)S(1)}, u32[]{:S(2)}) copy-start(bf16[128,32,128]{2,1,0:T(8,128)(2,1)S(1)} %broadcast_select_fusion.refs_5_.refs_6_) | copy-start | bytes 3145732
  59.3 13.3 %collective-permute-start.6 = (bf16[128,32,128]{2,1,0:T(8,128)(2,1)S(1)}, bf16[128,32,128]{2,1,0:T(8,128)(2,1)S(1)}, u32[]{:S(2)}, u32[]{:S(2)}) collective-permute-start(bf16[128,32,128]{2,1,0:T(8,128)(2,1)S(1)} %broadcast_select_fusion.refs_5_.refs_6_), channel_id=1, source_target_pairs={{0,4},{8,12},{5,1},{13,9},{2,6},{10,14},{7,3},{15,11},{16,20},{24,... | collective-permute-start | bytes 3145736 | tf_op jit(solution)/shard_map/ppermute | solution.py:300
  64.5 8.0 %copy-start.7 = (bf16[128,32,128]{2,1,0:T(8,128)(2,1)}, bf16[128,32,128]{2,1,0:T(8,128)(2,1)S(1)}, u32[]{:S(2)}) copy-start(bf16[128,32,128]{2,1,0:T(8,128)(2,1)S(1)} %collective-permute-done.1.refs_2_.refs_8_) | copy-start | bytes 3145732
  64.5 39.7 %collective-permute-start.10 = (bf16[128,32,128]{2,1,0:T(8,128)(2,1)S(1)}, bf16[128,32,128]{2,1,0:T(8,128)(2,1)S(1)}, u32[]{:S(2)}, u32[]{:S(2)}) collective-permute-start(bf16[128,32,128]{2,1,0:T(8,128)(2,1)S(1)} %collective-permute-done.1.refs_2_.refs_8_), channel_id=1, source_target_pairs={{0,12},{5,9},{10,6},{15,3},{16,28},{21,25},{26,22},{31,19}} | collective-permute-start | bytes 3145736 | tf_op jit(solution)/shard_map/ppermute | solution.py:305
  68.6 37.3 %collective-permute-start.9 = (bf16[128,32,128]{2,1,0:T(8,128)(2,1)S(1)}, bf16[128,32,128]{2,1,0:T(8,128)(2,1)S(1)}, u32[]{:S(2)}, u32[]{:S(2)}) collective-permute-start(bf16[128,32,128]{2,1,0:T(8,128)(2,1)S(1)} %collective-permute-done.1.refs_2_.refs_8_), channel_id=1, source_target_pairs={{0,8},{5,13},{10,2},{15,7},{16,24},{21,29},{26,18},{31,23}} | collective-permute-start | bytes 3145736 | tf_op jit(solution)/shard_map/ppermute | solution.py:305
  69.9 35.9 %collective-permute-start.8 = (bf16[128,32,128]{2,1,0:T(8,128)(2,1)S(1)}, bf16[128,32,128]{2,1,0:T(8,128)(2,1)}, u32[]{:S(2)}, u32[]{:S(2)}) collective-permute-start(bf16[128,32,128]{2,1,0:T(8,128)(2,1)S(1)} %collective-permute-done.1.refs_2_.refs_8_), channel_id=1, source_target_pairs={{0,4},{5,1},{10,14},{15,11},{16,20},{21,17},{26,30},{31,27}} | collective-permute-start | bytes 3145736 | tf_op jit(solution)/shard_map/ppermute | solution.py:305
  72.3 26.3 %collective-permute-start.4 = (bf16[128,32,128]{2,1,0:T(8,128)(2,1)S(1)}, bf16[128,32,128]{2,1,0:T(8,128)(2,1)S(1)}, u32[]{:S(2)}, u32[]{:S(2)}) collective-permute-start(bf16[128,32,128]{2,1,0:T(8,128)(2,1)S(1)} %collective-permute-done.1.refs_2_.refs_8_), channel_id=1, source_target_pairs={{0,3},{1,0},{2,1},{3,2},{4,7},{5,4},{6,5},{7,6},{8,11},{9,8},{10,9... | collective-permute-start | bytes 3145736 | tf_op jit(solution)/shard_map/ppermute | solution.py:363
  72.6 1.1 copy-start.11
  98.6 7.3 %copy-start.9 = (bf16[128,32,128]{2,1,0:T(8,128)(2,1)}, bf16[128,32,128]{2,1,0:T(8,128)(2,1)S(1)}, u32[]{:S(2)}) copy-start(bf16[128,32,128]{2,1,0:T(8,128)(2,1)S(1)} %collective-permute-done.4.refs_3_.refs_4_) | copy-start | bytes 3145732
  98.6 42.7 %collective-permute-start.12 = (bf16[128,32,128]{2,1,0:T(8,128)(2,1)S(1)}, bf16[128,32,128]{2,1,0:T(8,128)(2,1)S(1)}, u32[]{:S(2)}, u32[]{:S(2)}) collective-permute-start(bf16[128,32,128]{2,1,0:T(8,128)(2,1)S(1)} %collective-permute-done.4.refs_3_.refs_4_), channel_id=1, source_target_pairs={{0,12},{5,9},{10,6},{15,3},{16,28},{21,25},{26,22},{31,19}} | collective-permute-start | bytes 3145736 | tf_op jit(solution)/shard_map/ppermute | solution.py:305
  102.9 38.4 %collective-permute-start.11 = (bf16[128,32,128]{2,1,0:T(8,128)(2,1)S(1)}, bf16[128,32,128]{2,1,0:T(8,128)(2,1)S(1)}, u32[]{:S(2)}, u32[]{:S(2)}) collective-permute-start(bf16[128,32,128]{2,1,0:T(8,128)(2,1)S(1)} %collective-permute-done.4.refs_3_.refs_4_), channel_id=1, source_target_pairs={{0,8},{5,13},{10,2},{15,7},{16,24},{21,29},{26,18},{31,23}} | collective-permute-start | bytes 3145736 | tf_op jit(solution)/shard_map/ppermute | solution.py:305
  104.2 1.6 copy-start.15
  104.3 37.0 %collective-permute-start.7 = (bf16[128,32,128]{2,1,0:T(8,128)(2,1)S(1)}, bf16[128,32,128]{2,1,0:T(8,128)(2,1)S(1)}, u32[]{:S(2)}, u32[]{:S(2)}) collective-permute-start(bf16[128,32,128]{2,1,0:T(8,128)(2,1)S(1)} %collective-permute-done.4.refs_3_.refs_4_), channel_id=1, source_target_pairs={{0,4},{5,1},{10,14},{15,11},{16,20},{21,17},{26,30},{31,27}} | collective-permute-start | bytes 3145736 | tf_op jit(solution)/shard_map/ppermute | solution.py:305
  105.9 1.0 copy-start.16
  141.2 1.0 copy-start.12
  141.3 1.3 copy-start.13
  142.6 1.0 copy-start.14
